TPU v7x, 32 devices: a whole 2x2x4 slice. The times are simulated.
32 devices in a mesh: seq: 4 (over x, core), batch: 8 (over z, y).
Axes of the slice: x: 2, y: 2, z: 4, core: 2. Of those that a mesh axis runs over, the one named last changes fastest.
Arguments:
- inputs: bfloat16 [64, 512, 768], P('batch', 'seq'), may hold values from -6 to 6
- out_grad: float32 [64, 512, 768], P('batch', 'seq'), may hold values from -6 to 6
- out_mask: int32 [64, 512], P('batch', 'seq'), may hold values 0 or 1
- attn_mask: int32 [12, 512, 512], replicated, may hold values from 0 to 1, as said below
- mat_param: float32 [7077888], P(('seq', 'batch')), may hold values from -2 to 2
- mat_first: float32 [7077888], P(('seq', 'batch')), may hold values from -14 to 14
- mat_second: float32 [7077888], P(('seq', 'batch')), may hold values from 0.442368 to 1.769472
- vec_param: float32 [9216], P(('seq', 'batch')), may hold values from -1 to 2
- vec_first: float32 [9216], P(('seq', 'batch')), may hold values from -48 to 48
- vec_second: float32 [9216], P(('seq', 'batch')), may hold values from 4.9152 to 19.6608
Outputs:
- outputs: bfloat16 [64, 512, 768], P('batch', 'seq')
- input_grad: float32 [64, 512, 768], P('batch', 'seq')
- new_mats: float32 [7077888], P(('seq', 'batch'))
- new_mat_first: float32 [7077888], P(('seq', 'batch'))
- new_mat_second: float32 [7077888], P(('seq', 'batch'))
- new_vecs: float32 [9216], P(('seq', 'batch'))
- new_vec_first: float32 [9216], P(('seq', 'batch'))
- new_vec_second: float32 [9216], P(('seq', 'batch'))
Inputs may be any that keep to these rules, and one draw needn't show every extreme that they name: `attn_mask`: every head's mask is 1 on its diagonal.
All inputs are finite; a program needn't handle non-finite values. No bound on the sum of `out_mask` on one device may be relied on, other than what follows from the above.
Results may differ from a plain program's by a relative error of at most 0.013.
Values may be sent and summed in bfloat16 or wider, within the bound.
A program may use at most 192 MiB of HBM per device.

v0:
```python
import math

import jax
import jax.numpy as jnp
from jax import lax
from jax.sharding import PartitionSpec as P

D = 768
FF = 3072
STEP = 10


NEG_FILL = -1e30
NORM_EPS = 1e-06
ROOT_HALF = 0.7071067811865476
BETA_ONE = 0.9
BETA_TWO = 0.999
ADAM_EPS = 1e-08
DECAY_RATE = 0.01
MATS_RATE = 0.1
VECS_RATE = 0.5


def layer_norm(values, gain, shift):
    center = values - jnp.mean(values, -1, keepdims=True)
    spread = jnp.mean(center * center, -1, keepdims=True)
    return center * lax.rsqrt(spread + NORM_EPS) * gain + shift


def gelu_exact(values):
    return 0.5 * values * (1.0 + lax.erf(values * ROOT_HALF))


def unpack_mats(flat):
    first = 3 * D * D
    second = first + D * D
    third = second + D * FF
    return (
        flat[:first].reshape(D, 3 * D),
        flat[first:second].reshape(D, D),
        flat[second:third].reshape(D, FF),
        flat[third:].reshape(FF, D),
    )


def unpack_vecs(flat):
    pieces = []
    offset = 0
    for length in (D, D, D, FF, D, D, D, D, D):
        pieces.append(flat[offset : offset + length])
        offset = offset + length
    return pieces


def adam_step(param, first, second, grad, rate):
    first_new = BETA_ONE * first + (1.0 - BETA_ONE) * grad
    second_new = BETA_TWO * second + (1.0 - BETA_TWO) * grad * grad
    first_hat = first_new / (1.0 - BETA_ONE**STEP)
    second_hat = second_new / (1.0 - BETA_TWO**STEP)
    param_new = param - rate * (first_hat / (jnp.sqrt(second_hat) + ADAM_EPS) + DECAY_RATE * param)
    return (param_new, first_new, second_new)


def contract_rows(operand_one, operand_two):
    return lax.dot_general(
        operand_one, operand_two, (((0,), (0,)), ((), ())), preferred_element_type=jnp.float32
    )


def contract_cols(operand_one, operand_two):
    return lax.dot_general(
        operand_one, operand_two, (((1,), (1,)), ((), ())), preferred_element_type=jnp.float32
    )


def by_groups(function, arrays, group):
    blocks = arrays[0].shape[0] // group
    shaped = tuple((member.reshape((blocks, group) + member.shape[1:]) for member in arrays))
    result = lax.map(function, shaped)
    return jax.tree.map(lambda member: member.reshape((blocks * group,) + member.shape[2:]), result)


def local(
    inputs,
    out_grad,
    out_mask,
    attn_mask,
    mat_param,
    mat_first,
    mat_second,
    vec_param,
    vec_first,
    vec_second,
):
    seq_count, block_rows, model_width = inputs.shape
    heads = attn_mask.shape[0]
    head_size = model_width // heads
    tok_rows = seq_count * block_rows
    score_scale = 1.0 / math.sqrt(head_size)
    group = math.gcd(seq_count, max(1, 512 // block_rows))
    offset_rows = lax.axis_index("seq") * block_rows
    keep_rows = lax.dynamic_slice_in_dim(attn_mask, offset_rows, block_rows, 1) > 0
    mats_copy, vecs_copy = (
        lax.all_gather(mat_param.astype(jnp.bfloat16), ("seq", "batch"), axis=0, tiled=True),
        lax.all_gather(vec_param.astype(jnp.bfloat16), ("seq", "batch"), axis=0, tiled=True),
    )
    w_qkv, w_out, w_up, w_down = unpack_mats(mats_copy)
    (
        bias_query,
        bias_value,
        bias_out,
        bias_up,
        bias_down,
        gain_one,
        shift_one,
        gain_two,
        shift_two,
    ) = unpack_vecs(vecs_copy.astype(jnp.float32))
    flat_in = inputs.reshape(tok_rows, model_width)
    proj_cols = lax.dot_general(
        w_qkv, inputs, (((0,), (2,)), ((), ())), preferred_element_type=jnp.float32
    )
    proj_bias = jnp.concatenate([bias_query, jnp.zeros_like(bias_query), bias_value])
    proj_cols = (proj_cols + proj_bias[:, None, None]).astype(jnp.bfloat16)
    qkv_low = jnp.transpose(proj_cols, (1, 0, 2)).reshape(
        seq_count, 3, heads, head_size, block_rows
    )
    queries = qkv_low[:, 0]
    keys_own = qkv_low[:, 1]
    values_own = qkv_low[:, 2]
    keys_all, values_all = (
        lax.all_gather(keys_own, "seq", axis=3, tiled=True),
        lax.all_gather(values_own, "seq", axis=3, tiled=True),
    )

    def attend_forward(blocks):
        block_q, block_k, block_v = blocks
        scores = (
            jnp.einsum("bhdq,bhdk->bhqk", block_q, block_k, preferred_element_type=jnp.float32)
            * score_scale
        )
        scores = jnp.where(keep_rows, scores, NEG_FILL)
        largest = jnp.max(scores, -1, keepdims=True)
        expo = jnp.where(keep_rows, jnp.exp(scores - largest), 0.0)
        totals = jnp.sum(expo, -1, keepdims=True)
        probs = expo / totals
        mixed = jnp.einsum(
            "bhqk,bhdk->bhdq",
            probs.astype(jnp.bfloat16),
            block_v,
            preferred_element_type=jnp.float32,
        )
        return (mixed.astype(jnp.bfloat16), (largest + jnp.log(totals))[..., 0])

    attended, log_total = by_groups(attend_forward, (queries, keys_all, values_all), group)
    attended_cols = attended.reshape(seq_count, model_width, block_rows)
    attn_term = lax.dot_general(
        attended_cols, w_out, (((1,), (0,)), ((), ())), preferred_element_type=jnp.float32
    )
    first_sum = flat_in.astype(jnp.float32) + attn_term.reshape(tok_rows, model_width) + bias_out
    hidden_one = layer_norm(first_sum, gain_one, shift_one)
    hidden_low = hidden_one.astype(jnp.bfloat16)
    up_sum = jnp.dot(hidden_low, w_up, preferred_element_type=jnp.float32) + bias_up
    act_low = gelu_exact(up_sum).astype(jnp.bfloat16)
    second_sum = (
        hidden_one + jnp.dot(act_low, w_down, preferred_element_type=jnp.float32) + bias_down
    )
    result = layer_norm(second_sum, gain_two, shift_two)
    outputs = result.astype(jnp.bfloat16).reshape(seq_count, block_rows, model_width)
    grad_out = out_grad.reshape(tok_rows, model_width) * out_mask.reshape(tok_rows, 1).astype(
        jnp.float32
    )
    _, norm_two_back = jax.vjp(layer_norm, second_sum, gain_two, shift_two)
    grad_second, grad_gain_two, grad_shift_two = norm_two_back(grad_out)
    grad_down_low = grad_second.astype(jnp.bfloat16)
    grad_w_down = contract_rows(act_low, grad_down_low)
    grad_bias_down = jnp.sum(grad_down_low.astype(jnp.float32), 0)
    grad_act = contract_cols(grad_down_low, w_down)
    _, gelu_back = jax.vjp(gelu_exact, up_sum)
    grad_up_low = gelu_back(grad_act)[0].astype(jnp.bfloat16)
    grad_w_up = contract_rows(hidden_low, grad_up_low)
    grad_bias_up = jnp.sum(grad_up_low.astype(jnp.float32), 0)
    grad_hidden = grad_second + contract_cols(grad_up_low, w_up)
    _, norm_one_back = jax.vjp(layer_norm, first_sum, gain_one, shift_one)
    grad_first, grad_gain_one, grad_shift_one = norm_one_back(grad_hidden)
    grad_attn_low = grad_first.astype(jnp.bfloat16)
    grad_attn_rows = grad_attn_low.reshape(seq_count, block_rows, model_width)
    grad_w_out = lax.dot_general(
        attended_cols,
        grad_attn_rows,
        (((0, 2), (0, 1)), ((), ())),
        preferred_element_type=jnp.float32,
    )
    grad_bias_out = jnp.sum(grad_attn_low.astype(jnp.float32), 0)
    grad_mixed = lax.dot_general(
        w_out, grad_attn_rows, (((1,), (2,)), ((), ())), preferred_element_type=jnp.float32
    ).astype(jnp.bfloat16)
    grad_mixed = jnp.transpose(grad_mixed, (1, 0, 2)).reshape(
        seq_count, heads, head_size, block_rows
    )

    def attend_backward(blocks):
        block_q, block_k, block_v, block_g, block_lse = blocks
        scores = (
            jnp.einsum("bhdq,bhdk->bhqk", block_q, block_k, preferred_element_type=jnp.float32)
            * score_scale
        )
        probs = jnp.where(keep_rows, jnp.exp(scores - block_lse[..., None]), 0.0)
        grad_probs = jnp.einsum(
            "bhdq,bhdk->bhqk", block_g, block_v, preferred_element_type=jnp.float32
        )
        inner = jnp.sum(probs * grad_probs, -1, keepdims=True)
        grad_scores = (probs * (grad_probs - inner)).astype(jnp.bfloat16)
        grad_q = (
            jnp.einsum("bhqk,bhdk->bhdq", grad_scores, block_k, preferred_element_type=jnp.float32)
            * score_scale
        )
        grad_k = (
            jnp.einsum("bhqk,bhdq->bhdk", grad_scores, block_q, preferred_element_type=jnp.float32)
            * score_scale
        )
        grad_v = jnp.einsum(
            "bhqk,bhdq->bhdk",
            probs.astype(jnp.bfloat16),
            block_g,
            preferred_element_type=jnp.float32,
        )
        return (grad_q, grad_k, grad_v)

    grad_queries, key_terms, value_terms = by_groups(
        attend_backward, (queries, keys_all, values_all, grad_mixed, log_total), group
    )
    grad_keys, grad_values = (
        lax.psum_scatter(
            key_terms.astype(jnp.bfloat16), "seq", scatter_dimension=3, tiled=True
        ).astype(jnp.float32),
        lax.psum_scatter(
            value_terms.astype(jnp.bfloat16), "seq", scatter_dimension=3, tiled=True
        ).astype(jnp.float32),
    )
    grad_proj = jnp.concatenate(
        [
            grad_queries.reshape(seq_count, model_width, block_rows),
            grad_keys.reshape(seq_count, model_width, block_rows),
            grad_values.reshape(seq_count, model_width, block_rows),
        ],
        1,
    )
    grad_proj_low = grad_proj.astype(jnp.bfloat16)
    grad_w_qkv = lax.dot_general(
        inputs, grad_proj_low, (((0, 1), (0, 2)), ((), ())), preferred_element_type=jnp.float32
    )
    proj_sums = jnp.sum(grad_proj_low.astype(jnp.float32), (0, 2))
    grad_bias_query = proj_sums[:model_width]
    grad_bias_value = proj_sums[2 * model_width :]
    back_term = lax.dot_general(
        grad_proj_low, w_qkv, (((1,), (1,)), ((), ())), preferred_element_type=jnp.float32
    )
    input_grad = grad_first + back_term.reshape(tok_rows, model_width)
    grad_mats = jnp.concatenate(
        [
            grad_w_qkv.reshape(-1),
            grad_w_out.reshape(-1),
            grad_w_up.reshape(-1),
            grad_w_down.reshape(-1),
        ]
    )
    grad_vecs = jnp.concatenate(
        [
            grad_bias_query,
            grad_bias_value,
            grad_bias_out,
            grad_bias_up,
            grad_bias_down,
            grad_gain_one,
            grad_shift_one,
            grad_gain_two,
            grad_shift_two,
        ]
    )
    mats_share, vecs_share = (
        lax.psum_scatter(grad_mats, ("seq", "batch"), scatter_dimension=0, tiled=True),
        lax.psum_scatter(grad_vecs, ("seq", "batch"), scatter_dimension=0, tiled=True),
    )
    new_mats, new_mat_first, new_mat_second = adam_step(
        mat_param, mat_first, mat_second, mats_share, MATS_RATE
    )
    new_vecs, new_vec_first, new_vec_second = adam_step(
        vec_param, vec_first, vec_second, vecs_share, VECS_RATE
    )
    return (
        outputs,
        input_grad.reshape(seq_count, block_rows, model_width),
        new_mats,
        new_mat_first,
        new_mat_second,
        new_vecs,
        new_vec_first,
        new_vec_second,
    )


def solution(mesh):
    placed = (
        P("batch", "seq", None),
        P("batch", "seq", None),
        P("batch", "seq"),
        P(),
        P(("seq", "batch")),
        P(("seq", "batch")),
        P(("seq", "batch")),
        P(("seq", "batch")),
        P(("seq", "batch")),
        P(("seq", "batch")),
    )
    return jax.shard_map(
        local,
        mesh=mesh,
        in_specs=placed,
        out_specs=(
            P("batch", "seq", None),
            P("batch", "seq", None),
            P(("seq", "batch")),
            P(("seq", "batch")),
            P(("seq", "batch")),
            P(("seq", "batch")),
            P(("seq", "batch")),
            P(("seq", "batch")),
        ),
        check_vma=False,
    )
```

profile of v0, /device:TPU:0, one launch (start us, length us, event | category | flops | bytes accessed | tf_op | source)
XLA Modules:
  0.0 1066.4 jit_solution(2391243824348619873)
XLA Ops:
  10.2 42.9 %all-reduce = bf16[9216]{0:T(1024)(128)(2,1)S(1)} all-reduce(bf16[9216]{0:T(1024)(128)(2,1)S(1)} %dynamic-update-slice), channel_id=1, replica_groups=mesh['seq'=4,'batch'=8] {'seq','batch'}, use_global_device_ids=true, to_apply=%add | all-reduce | flops 9216 | bytes 36864
  53.6 64.8 %all-gather.6.cloned.1.call-done = bf16[7077888]{0:T(1024)(128)(2,1)} async-done(((bf16[221184]{0:T(1024)(128)(2,1)}), bf16[7077888]{0:T(1024)(128)(2,1)}) %all-gather.6.cloned.1.call-update) | async-done | bytes 14155792 | tf_op jit(solution)/shard_map/all_gather | solution.py:104
  121.8 7.7 slice.95
  129.5 6.6 add_convert_fusion.1
  142.8 8.9 fusion.76
  156.8 9.3 slice.110
  166.1 8.3 slice.107
  174.3 10.0 all-gather.10.cloned.1.call-done
  184.4 49.4 %all-gather.8.cloned.1.call-done = bf16[8,1,12,64,512]{4,3,2,1,0:T(8,128)(2,1)} async-done(((bf16[8,1,12,64,128]{4,3,2,1,0:T(8,128)(2,1)}), bf16[8,1,12,64,512]{4,3,2,1,0:T(8,128)(2,1)}) %all-gather.8.cloned.1.call-update) | async-done | bytes 6291472 | tf_op jit(solution)/shard_map/all_gather | solution.py:133
  233.8 33.6 %while.26 = (s32[]{:T(128)}, bf16[2,4,12,64,128]{4,3,2,1,0:T(8,128)(2,1)}, f32[2,4,12,128]{3,2,1,0:T(8,128)}, bf16[2,4,12,64,512]{4,3,2,1,0:T(8,128)(2,1)}, pred...) while((s32[]{:T(128)}, ...), condition=%wide.region_3.4_spmd, body=%wide.region_0.3_spmd.sunk | while | flops 849733632 | bytes 86354160 | solution.py:79
  233.8 4.5 fusion.119
  238.2 4.7 fusion.120
  242.9 5.8 fusion.121
  250.6 4.4 fusion.119
  255.0 4.7 fusion.120
  259.7 5.8 fusion.121
  274.2 9.7 multiply_convert_fusion.1
  286.5 5.4 fusion.81
  300.0 15.0 %convert_reduce_fusion = (f32[3072]{0:T(1024)}, bf16[1024,3072]{1,0:T(8,128)(2,1)S(1)}) fusion(bf16[1024,768]{1,0:T(8,128)(2,1)S(1)} %get-tuple-element.158, bf16[3072,768]{1,0:T(8,128)(2,1)S(1)} %bitcast.191, f32[1024,3072]{1,0:T(8,128)} %get-tuple-element.191, f32[3072]{0:T(1024)S(1)} %copy-done.43), kind=kOutput, calls=%fused_computation.60 | convolution fusion | flops 4882166784 | bytes 25190400 | tf_op jit(solution)/shard_map/dot_general | solution.py:71
  315.0 8.2 multiply_reduce_fusion.3
  335.0 63.4 %while.27 = (s32[]{:T(128)}, bf16[2,4,12,64,128]{4,3,2,1,0:T(8,128)(2,1)}, bf16[2,4,12,64,512]{4,3,2,1,0:T(8,128)(2,1)}, bf16[2,4,12,64,512]{4,3,2,1,0:T(8,128)(...) while((s32[]{:T(128)}, ...), condition=%wide.region_14.15_spmd, body=%wide.region_12.14_spmd.sunk | while | flops 2062411776 | bytes 142537936 | solution.py:79
  339.1 4.7 bitcast_dynamic-update-slice_fusion.11
  343.8 9.1 multiply_reduce_fusion.9
  352.9 7.0 multiply_convert_fusion.3
  370.8 4.7 bitcast_dynamic-update-slice_fusion.11
  375.5 9.1 multiply_reduce_fusion.9
  384.6 7.0 multiply_convert_fusion.3
  398.5 23.7 %copy.39 = bf16[8,12,64,512]{2,1,0,3:T(8,128)(2,1)} copy(bf16[8,12,64,512]{3,2,1,0:T(8,128)(2,1)} %bitcast.188) | data formatting | bytes 12582912
  422.1 21.4 %reshape.241 = bf16[512,6144]{1,0:T(8,128)(2,1)} reshape(bf16[512,8,12,64]{3,2,1,0:T(8,128)(2,1)} %bitcast.172) | data formatting | bytes 12582912
  443.6 23.7 %copy.37 = bf16[8,12,64,512]{2,1,0,3:T(8,128)(2,1)} copy(bf16[8,12,64,512]{3,2,1,0:T(8,128)(2,1)} %bitcast.189) | data formatting | bytes 12582912
  467.3 21.4 %reshape.239 = bf16[512,6144]{1,0:T(8,128)(2,1)} reshape(bf16[512,8,12,64]{3,2,1,0:T(8,128)(2,1)} %bitcast.173) | data formatting | bytes 12582912
  489.4 9.1 convolution_bitcast_fusion.1
  498.6 5.9 copy.41
  510.6 10.8 %fusion.82 = f32[3072,768]{1,0:T(8,128)} fusion(bf16[1024,3072]{1,0:T(8,128)(2,1)} %copy-done.53, bf16[1024,768]{1,0:T(8,128)(2,1)S(1)} %copy-done.15), kind=kOutput, calls=%fused_computation.136 | convolution fusion | flops 4831838208 | bytes 17301504 | tf_op jit(solution)/shard_map/dot_general | solution.py:65
  521.4 10.8 %reshape.226 = f32[2359296]{0:T(1024)} reshape(f32[3072,768]{1,0:T(8,128)} %fusion.82) | data formatting | bytes 18874368 | tf_op jit(solution)/shard_map/reshape | solution.py:265
  532.3 6.2 reshape.242
  538.5 5.1 copy.40
  543.6 19.4 %reduce-scatter.7.cloned.1.call-done = bf16[128,6144]{1,0:T(8,128)(2,1)} async-done(((bf16[512,6144]{1,0:T(8,128)(2,1)}), bf16[128,6144]{1,0:T(8,128)(2,1)}) %reduce-scatter.7.cloned.1.call-update) | async-done | bytes 1572880
  563.0 6.2 reshape.240
  569.2 5.1 copy.38
  574.3 9.0 convolution_bitcast_fusion
  583.3 8.1 copy.34
  591.3 7.9 reshape.223
  599.2 26.5 %pad_maximum_fusion = f32[7077888]{0:T(1024)} fusion(f32[2359296]{0:T(1024)} %reshape.226, f32[2359296]{0:T(1024)} %bitcast.176, f32[589824]{0:T(1024)} %reshape.224, f32[1769472]{0:T(1024)} %reshape.223), kind=kLoop, calls=%fused_computation.59 | loop fusion | flops 21233664 | bytes 56623104 | tf_op jit(solution)/shard_map/concatenate | solution.py:260
  630.9 6.9 copy.33
  640.1 41.4 %all-reduce.2 = f32[9216]{0:T(1024)S(1)} all-reduce(f32[9216]{0:T(1024)S(1)} %constant_dynamic-update-slice_fusion), channel_id=7, replica_groups=mesh['seq'=4,'batch'=8] {'seq','batch'}, use_global_device_ids=true, to_apply=%region_26.27.clone | all-reduce | flops 9216 | bytes 73728
  682.2 10.3 add_add_fusion.3
  692.5 363.5 %all-reduce.5.cloned.1.call-done = f32[7077888]{0:T(1024)} async-done(((f32[7077888]{0:T(1024)}), f32[7077888]{0:T(1024)}) %all-reduce.5.cloned.1.call-update) | async-done | bytes 28311568
  (208 shorter events, 90.9 us)
Async XLA Ops:
  7.2 111.3 %all-gather.6.cloned.1.call-start = ((), (), s32[]{:S(2)}) async-start(), calls=%async_computation.2 | async-start | bytes 14598144 | tf_op jit(solution)/shard_map/all_gather | solution.py:104
  9.2 175.2 %all-gather.10.cloned.1.call-start = ((), (), s32[]{:S(2)}) async-start(), calls=%async_computation.4 | async-start | bytes 7864320 | tf_op jit(solution)/shard_map/all_gather | solution.py:132
  121.8 7.7 copy-start.52
  138.8 3.0 copy-start.45
  138.9 94.9 %all-gather.8.cloned.1.call-start = ((), (), s32[]{:S(2)}) async-start(), calls=%async_computation.3 | async-start | bytes 7864320 | tf_op jit(solution)/shard_map/all_gather | solution.py:133
  142.5 389.8 %reduce-scatter.9.cloned.1.call-start = ((), (), s32[]{:S(2)}) async-start(), calls=%async_computation.6 | async-start | bytes 7864320
  233.8 36.1 %copy-start.19 = (bf16[768,768]{1,0:T(8,128)(2,1)S(1)}, bf16[768,768]{1,0:T(8,128)(2,1)}, u32[]{:S(2)}) copy-start(bf16[768,768]{1,0:T(8,128)(2,1)} %slice.102) | copy-start | bytes 3538948
  233.8 36.1 %copy-start.47 = (f32[768]{0:T(1024)S(1)}, f32[768]{0:T(1024)}, u32[]{:S(2)}) copy-start(f32[768]{0:T(1024)} %get-tuple-element.183) | copy-start | bytes 9220
  238.2 4.7 copy-start.1
  238.2 4.7 copy-start.11
  242.9 5.8 copy-start.22
  255.0 4.7 copy-start.1
  255.0 4.7 copy-start.11
  259.7 5.8 copy-start.22
  269.9 4.2 copy-start.9
  269.9 4.2 copy-start.29
  269.9 4.2 copy-start.31
  269.9 4.2 copy-start.43
  273.5 49.7 %copy-start.2 = (f32[1024,768]{1,0:T(8,128)}, f32[1024,768]{1,0:T(8,128)S(1)}, u32[]{:S(2)}) copy-start(f32[1024,768]{1,0:T(8,128)S(1)} %get-tuple-element.189) | copy-start | bytes 9437188
  273.5 49.7 %copy-start.25 = (f32[1024]{0:T(1024)}, f32[1024]{0:T(1024)S(1)}, u32[]{:S(2)}) copy-start(f32[1024]{0:T(1024)S(1)} %broadcast_multiply_fusion.1) | copy-start | bytes 12292
  273.5 13.0 %slice-start = ((s8[4718592]{0:T(1024)(128)(4,1)}), s8[4194304]{0:T(1024)(128)(4,1)S(1)}, s32[]{:S(2)}) async-start(s8[4718592]{0:T(1024)(128)(4,1)} %bitcast.190), calls=%async_computation.8 | async-start | bytes 8388608
  274.1 49.1 %copy-start.27 = (f32[1024]{0:T(1024)}, f32[1024]{0:T(1024)S(1)}, u32[]{:S(2)}) copy-start(f32[1024]{0:T(1024)S(1)} %fusion.65) | copy-start | bytes 12292
  274.1 12.4 %slice-start.1 = ((s8[4718592]{0:T(1024)(128)(4,1)}), s8[524288]{0:T(1024)(128)(4,1)S(1)}, s32[]{:S(2)}) async-start(s8[4718592]{0:T(1024)(128)(4,1)} %bitcast.190), calls=%async_computation.9 | async-start | bytes 1048576
  274.1 12.4 %copy-start.46 = (f32[768]{0:T(1024)S(1)}, f32[768]{0:T(1024)}, u32[]{:S(2)}) copy-start(f32[768]{0:T(1024)} %get-tuple-element.180) | copy-start | bytes 9220
  286.5 6.0 copy-start.33
  286.5 6.0 copy-start.34
  292.5 3.6 copy-start.36
  300.0 15.0 %copy-start.14 = (bf16[1024,768]{1,0:T(8,128)(2,1)}, bf16[1024,768]{1,0:T(8,128)(2,1)S(1)}, u32[]{:S(2)}) copy-start(bf16[1024,768]{1,0:T(8,128)(2,1)S(1)} %get-tuple-element.158) | copy-start | bytes 4718596
  315.0 8.2 copy-start.5
  326.1 3.8 copy-start.18
  329.9 5.2 copy-start.24
  335.2 3.9 copy-start
  352.9 7.0 copy-start.6
  366.9 3.9 copy-start
  384.6 7.0 copy-start.6
  443.5 119.5 %reduce-scatter.7.cloned.1.call-start = ((), (), s32[]{:S(2)}) async-start(), calls=%async_computation.5 | async-start | bytes 7864320
  488.7 567.3 %all-reduce.5.cloned.1.call-start = ((), (), s32[]{:S(2)}) async-start(), calls=%async_computation.7 | async-start | bytes 56623104
  498.5 5.9 copy-start.13
  498.5 5.9 copy-start.17
  507.3 3.3 copy-start.15
  625.8 2.8 copy-start.8
  637.9 43.5 %copy-start.44 = (f32[288]{0:T(512)S(1)}, f32[288]{0:T(512)}, u32[]{:S(2)}) copy-start(f32[288]{0:T(512)} %param.21) | copy-start | bytes 3460
  637.9 43.5 %copy-start.50 = (f32[288]{0:T(512)S(1)}, f32[288]{0:T(512)}, u32[]{:S(2)}) copy-start(f32[288]{0:T(512)} %param.22) | copy-start | bytes 3460
  637.9 43.5 %copy-start.51 = (f32[288]{0:T(512)S(1)}, f32[288]{0:T(512)}, u32[]{:S(2)}) copy-start(f32[288]{0:T(512)} %param.23) | copy-start | bytes 3460
  637.9 44.2 %copy-start.39 = (f32[1024]{0:T(1024)S(1)}, f32[1024]{0:T(1024)}, u32[]{:S(2)}) copy-start(f32[1024]{0:T(1024)} %copy-done.38) | copy-start | bytes 12292
  682.1 373.9 %copy-start.10 = (f32[221184]{0:T(1024)S(1)}, f32[221184]{0:T(1024)}, u32[]{:S(2)}) copy-start(f32[221184]{0:T(1024)} %param.18) | copy-start | bytes 2654212
  682.1 373.9 %copy-start.20 = (f32[221184]{0:T(1024)S(1)}, f32[221184]{0:T(1024)}, u32[]{:S(2)}) copy-start(f32[221184]{0:T(1024)} %param.19) | copy-start | bytes 2654212
  682.1 373.9 %copy-start.21 = (f32[221184]{0:T(1024)S(1)}, f32[221184]{0:T(1024)}, u32[]{:S(2)}) copy-start(f32[221184]{0:T(1024)} %param.20) | copy-start | bytes 2654212
  (22 other events, 34.8 us)
Sparse Core Ops, SparseCore 0:
  11.5 106.8 all-gather.5
  139.0 45.3 all-gather.9
  186.5 47.2 all-gather.7
  443.6 58.3 reduce-scatter.8
  504.6 58.3 reduce-scatter.6
  625.9 430.0 all-reduce.4
where the time goes:
time: 1080 us; the launch traced here: 1070 us
  waiting for transfers between devices  507 us (47%)
  local copies, waits for them, and re-layouts  219 us (20%)
  matrix products  163 us (15%)
  blocking collectives  84.2 us (8%)
  other arithmetic  76.6 us (7%)
  between operations  15.2 us (1%)
    unnamed x9, waiting for transfers between devices  383 us
    unnamed x115, local copies, waits for them, and re-layouts  127 us
    unnamed x2, blocking collectives  84.2 us
    all_gather x1, waiting for transfers between devices, local(): lax.all_gather(mat_param.astype(jnp.bfloat16), ('seq', 'batch'), axis=0,...  64.8 us
    all_gather x1, waiting for transfers between devices, local(): lax.all_gather(values_own, 'seq', axis=3, tiled=True)  49.4 us
    concatenate x1, other arithmetic, local(): jnp.concatenate([grad_w_qkv.reshape(-1), grad_w_out.reshape(-1), grad_w_u...  26.5 us
    dot_general x2, matrix products, contract_cols(): lax.dot_general(operand_one, operand_two, (((1,), (1,)), ((), ())), prefe...  23.2 us
  transfers between devices with their start and end apart: 6, of which 5 were waited for; matrix products, arithmetic and copies ran while one was open for 15% of the time, Pallas kernels for 0%

commit v1 on v0

v1 whole, which is shorter than its diff:
```python
import functools
import math

import jax
import jax.numpy as jnp
from jax import lax
from jax.experimental import pallas as pl
from jax.experimental.pallas import tpu as pltpu
from jax.sharding import PartitionSpec as P

D = 768
FF = 3072
STEP = 10


NEG_FILL = -1e30
NORM_EPS = 1e-06
ROOT_HALF = 0.7071067811865476
ROOT_TWO_PI_INV = 0.3989422804014327
BETA_ONE = 0.9
BETA_TWO = 0.999
ADAM_EPS = 1e-08
DECAY_RATE = 0.01
MATS_RATE = 0.1
VECS_RATE = 0.5

BF16 = jnp.bfloat16
F32 = jnp.float32
MESH = pl.DeviceIdType.MESH
ANY = pl.BlockSpec(memory_space=pl.ANY)
VMEM = pl.BlockSpec(memory_space=pltpu.VMEM)
MIB = 1 << 20

MATRICES = (("qkv", 3 * D, 3), ("out", D, 1), ("up", FF, FF // D), ("down", FF, 1))
VEC_LENGTHS = (D, D, D, FF, D, D, D, D, D)


def layer_norm(values, gain, shift):
    center = values - jnp.mean(values, -1, keepdims=True)
    spread = jnp.mean(center * center, -1, keepdims=True)
    return center * lax.rsqrt(spread + NORM_EPS) * gain + shift


def gelu_exact(values):
    return 0.5 * values * (1.0 + lax.erf(values * ROOT_HALF))


def adam_step(param, first, second, grad, rate):
    first_new = BETA_ONE * first + (1.0 - BETA_ONE) * grad
    second_new = BETA_TWO * second + (1.0 - BETA_TWO) * grad * grad
    first_hat = first_new / (1.0 - BETA_ONE**STEP)
    second_hat = second_new / (1.0 - BETA_TWO**STEP)
    param_new = param - rate * (first_hat / (jnp.sqrt(second_hat) + ADAM_EPS) + DECAY_RATE * param)
    return (param_new, first_new, second_new)


def contract_rows(operand_one, operand_two):
    return lax.dot_general(
        operand_one, operand_two, (((0,), (0,)), ((), ())), preferred_element_type=jnp.float32
    )


def contract_cols(operand_one, operand_two):
    return lax.dot_general(
        operand_one, operand_two, (((1,), (1,)), ((), ())), preferred_element_type=jnp.float32
    )


def segments(share, rows):
    found, start = [], 0
    for name, length, pieces in MATRICES:
        low, high = max(start, share * rows), min(start + length, (share + 1) * rows)
        if low < high:
            found.append((name, pieces, low - share * rows, low - start, high - low))
        start += length
    return found


def by_columns(name, block, pieces):
    rows = block.shape[0]
    if name == "qkv":
        return block.reshape(rows // 3, 3, 3, D // 3).transpose(2, 0, 1, 3).reshape(rows, D)
    return block.reshape(rows // pieces, pieces, D).swapaxes(0, 1).reshape(rows, D)


def by_rows(name, block, pieces):
    rows = block.shape[0]
    if name == "qkv":
        return block.reshape(3, rows // 3, 3, D // 3).transpose(1, 2, 0, 3).reshape(rows, D)
    return block.reshape(pieces, rows // pieces, D).swapaxes(0, 1).reshape(rows, D)


def regroup(blocks):
    return blocks.reshape(3, D, 3, D // 3).transpose(2, 1, 0, 3).reshape(3, D, D)


def rearrange(share_index, shares, block, change):
    rows = block.shape[0]
    layouts, starts = [], []
    for share in range(shares):
        layout = tuple((name, pieces, at, size) for name, pieces, at, _, size in segments(share, rows))
        if not layouts or layout != layouts[-1]:
            layouts.append(layout)
            starts.append(share)

    def branch(layout, values):
        return jnp.concatenate([change(name, values[at : at + size], pieces) for name, pieces, at, size in layout])

    return lax.switch(
        sum((share_index >= start).astype(jnp.int32) for start in starts[1:]),
        [functools.partial(branch, layout) for layout in layouts],
        block,
    )


def take_matrix(gathered, name):
    shares, rows, _ = gathered.shape
    found = []
    for share in range(shares):
        for other, pieces, at, _, size in segments(share, rows):
            if other == name:
                found.append(gathered[share, at : at + size].reshape(pieces, size // pieces, D))
    return jnp.concatenate(found, 1)


def to_shares(blocks, shares):
    rows = sum(length for _, length, _ in MATRICES) // shares
    found = []
    for share in range(shares):
        for name, pieces, _, begin, size in segments(share, rows):
            part = blocks[name][:, begin // pieces : (begin + size) // pieces]
            found.append(part.reshape(size, D))
    return jnp.concatenate(found).reshape(shares, rows, D)


class Place:
    def __init__(self, n_batch):
        self.n_batch, self.n_z = n_batch, n_batch // 2
        self.seq, self.batch = lax.axis_index("seq"), lax.axis_index("batch")
        self.x, self.core = self.seq // 2, self.seq % 2
        self.z, self.y = self.batch // 2, self.batch % 2
        self.x_peer = {"seq": (1 - self.x) * 2 + self.core}
        self.core_peer = {"seq": self.x * 2 + 1 - self.core}
        self.y_peer = {"batch": self.z * 2 + 1 - self.y}
        self.ring = 2 * self.n_z
        self.position = (1 - self.y) * self.z + self.y * (self.ring - 1 - self.z)
        self.next, self.prev = {"batch": self.around(1)}, {"batch": self.around(-1)}

    def around(self, step):
        place = (self.position + step + self.ring) % self.ring
        y = place // self.n_z
        return 2 * ((1 - y) * place + y * (self.ring - 1 - place)) + y

    def share(self, x, core, step):
        return (2 * x + core) * self.n_batch + self.around(step)

    def z_at(self, step):
        return (self.z + step) % self.n_z

    def z_peer(self, step):
        return {"batch": self.z_at(step) * 2 + self.y}

    def seq_at(self, step):
        return (self.seq + step) % 4

    def seq_peer(self, step):
        return {"seq": self.seq_at(step)}

    def barrier(self):
        barrier = pltpu.get_barrier_semaphore()
        peers = [self.seq_peer(step) for step in (1, 2, 3)]
        peers += [self.y_peer] + [self.z_peer(step) for step in range(1, self.n_z)]
        for peer in peers:
            pl.semaphore_signal(barrier, inc=1, device_id=peer, device_id_type=MESH)
        pl.semaphore_wait(barrier, len(peers))


def run(steps):
    for step in steps:
        step()


def dispatch(now, steps, body):
    if len(steps) == 1:
        pl.when(now == steps[0])(functools.partial(body, steps[0]))
    elif steps:
        middle = len(steps) // 2
        lax.cond(
            now < steps[middle],
            lambda: dispatch(now, steps[:middle], body),
            lambda: dispatch(now, steps[middle:], body),
        )


class Sends:
    def __init__(self, sems):
        self.sems, self.started, self.when = sems, [], None

    def start(self, src, dst, recv_sem, peer, like=None):
        copy = pltpu.make_async_remote_copy(
            src_ref=src,
            dst_ref=dst,
            send_sem=self.sems.at[len(self.started)],
            recv_sem=recv_sem,
            device_id=peer,
            device_id_type=MESH,
        )
        copy.start()
        self.started.append((self.when, like or (lambda: src)))

    def arrived(self, dst, recv_sem, peer):
        pltpu.make_async_remote_copy(
            src_ref=dst,
            dst_ref=dst,
            send_sem=self.sems.at[0],
            recv_sem=recv_sem,
            device_id=peer,
            device_id_type=MESH,
        ).wait_recv()

    def sent(self, last, count, peer):
        for index in range(len(self.started) - last, len(self.started) - last + count):
            self.wait(index, self.started[index][1](), peer)
            self.started[index] = None

    def wait(self, index, ref, peer):
        pltpu.make_async_remote_copy(
            src_ref=ref,
            dst_ref=ref,
            send_sem=self.sems.at[index],
            recv_sem=self.sems.at[index],
            device_id=peer,
            device_id_type=MESH,
        ).wait_send()

    def under(self, condition, body):
        outer = self.when
        self.when = condition if outer is None else jnp.logical_and(outer, condition)

        @pl.when(condition)
        def _():
            body()

        self.when = outer

    def drain(self, peer):
        assert len(self.started) <= self.sems.shape[0]
        for index, (when, like) in [(i, one) for i, one in enumerate(self.started) if one]:
            if when is None:
                self.wait(index, like(), peer)
            else:
                pl.when(when)(lambda: self.wait(index, like(), peer))


def contract(one, two, dims):
    return lax.dot_general(one, two, ((dims[:1], dims[1:]), ((), ())), preferred_element_type=F32)


def half_of(shape, head):
    return lax.broadcasted_iota(jnp.int32, shape, 1) // 64 == head % 2


def row_of(grid, first, count):
    return jnp.concatenate([grid[first + i : first + i + 1, :] for i in range(count)], 1)


def attend_head(head, seq, qkv, mask, att, lse):
    lanes = pl.ds(pl.multiple_of(head // 2 * 128, 128), 128)
    length = mask.shape[0]
    block = 256
    k = qkv[1, seq, :, lanes]
    v = qkv[2, seq, :, lanes]
    v = jnp.where(half_of(v.shape, head), v, 1.0).astype(BF16)
    for i in range(length // block):
        rows = pl.ds(i * block, block)
        q = qkv[0, seq, rows, lanes]
        q = jnp.where(half_of(q.shape, head), q * 0.125, 0.0).astype(BF16)
        scores = contract(q, k, (1, 1))
        scores = jnp.where(mask[rows, :] > 0, scores, NEG_FILL)
        largest = jnp.max(scores, -1, keepdims=True)
        both = contract(jnp.exp(scores - largest).astype(BF16), v, (1, 0))
        turned = pltpu.roll(both, 64, 1)
        old = att[seq, rows, lanes]
        att[seq, rows, lanes] = jnp.where(half_of(old.shape, head), (both / turned).astype(BF16), old)
        total = jnp.where(head % 2 == 0, turned, both)
        kept = lse[seq, rows, :]
        lane = lax.broadcasted_iota(jnp.int32, kept.shape, 1)
        lse[seq, rows, :] = jnp.where(lane == head, largest + jnp.log(total), kept)


def head_backward(head, seq, qkv, mask, att, datt, lse, probs, dscore, dqkv):
    lanes = pl.ds(pl.multiple_of(head // 2 * 128, 128), 128)
    length = mask.shape[0]
    block = 256
    k = qkv[1, seq, :, lanes]
    v = qkv[2, seq, :, lanes]
    own = half_of(k.shape, head)
    k_own = jnp.where(own, k, 0.0).astype(BF16)
    for i in range(length // block):
        rows = pl.ds(i * block, block)
        q = qkv[0, seq, rows, lanes]
        g = datt[seq, rows, lanes]
        half = half_of(q.shape, head)
        q = jnp.where(half, q * 0.125, 0.0).astype(BF16)
        g = jnp.where(half, g, 0.0).astype(BF16)
        kept = lse[seq, rows, :]
        lane = lax.broadcasted_iota(jnp.int32, kept.shape, 1)
        total = jnp.sum(jnp.where(lane == head, kept, 0.0), -1, keepdims=True)
        inner = jnp.sum(g.astype(F32) * att[seq, rows, lanes].astype(F32), -1, keepdims=True)
        scores = contract(q, k, (1, 1))
        p = jnp.where(mask[rows, :] > 0, jnp.exp(scores - total), 0.0)
        d = p * (contract(g, v, (1, 1)) - inner)
        probs[rows, :] = p.astype(BF16)
        d = d.astype(BF16)
        dscore[rows, :] = d
        dq = contract(d, k_own, (1, 0)) * 0.125
        old = dqkv[0, seq, rows, lanes]
        dqkv[0, seq, rows, lanes] = jnp.where(half, dq.astype(BF16), old)
    q = qkv[0, seq, :, lanes]
    g = datt[seq, :, lanes]
    dk = contract(q.T, dscore[...], (1, 0)).T * 0.125
    dv = contract(g.T, probs[...], (1, 0)).T
    for j, value in ((1, dk), (2, dv)):
        old = dqkv[j, seq, :, lanes]
        dqkv[j, seq, :, lanes] = jnp.where(own, value.astype(BF16), old)


def add_rows(target, target_rows, *others):
    step = 32
    first, size = target_rows

    def body(i, carry):
        at = pl.ds(pl.multiple_of(first + i * step, 16), step)
        total = target[at].astype(F32)
        for ref, begin in others:
            total = total + ref[pl.ds(pl.multiple_of(begin + i * step, 16), step)].astype(F32)
        target[at] = total.astype(target.dtype)
        return carry

    lax.fori_loop(0, size // step, body, 0)


def norm_parts(values):
    center = values - jnp.mean(values, -1, keepdims=True)
    scale = lax.rsqrt(jnp.mean(center * center, -1, keepdims=True) + NORM_EPS)
    return center * scale, scale


def norm_back(grad, normed, scale, gain):
    dn = grad * gain
    along = jnp.mean(dn * normed, -1, keepdims=True)
    return (dn - jnp.mean(dn, -1, keepdims=True) - normed * along) * scale


BEFORE_UP, LAST_STEP = 72, 89
ACROSS_ORDER = (0, 1, -1, 2, -2, 3, -3, 4)
FIRST = {
    0: (("q", 1, 0), ("q_start", 1), ("q", 2, 0), ("q", 1, 1), ("q_start", 2), ("q", 3, 0), ("q", 2, 1), ("q", 1, 2), ("q", 4, 0)),
    2: (("q", 1, 0), ("q", 2, 0), ("q_start", 1), ("q", 3, 0), ("q", 1, 1), ("q", 4, 0)),
}
THEN = {
    0: (("q", 3, 1), ("q", 2, 2), ("q", 4, 1), ("q", 3, 2), ("q", 4, 2)),
    2: (("q", 2, 1), ("q_start", 2), ("q", 3, 1), ("q", 1, 2), ("q", 4, 1), ("q", 2, 2), ("q", 3, 2), ("q", 4, 2)),
}
TIMES = {
    0: dict(then=(0, 3, 4, 9, 89), far=(37, 49, 58, 66, 74), across=(0, 25, 30, 64, 80), dy=33),
    1: dict(own=(-1, 18, 24, 56, 64), over_x=0, far=(34, 43, 68, 76, 83), dy=27),
    2: dict(then=(0, 0, 0, 0, 11, 12, 17, 84), own=(1, 18, 27, 49, 57), over_x=0, dy=64),
    3: dict(own=(59, 69, 75, 83, 85), over_x=2, far=(3, 28, 43, 68, 76), across=(16, 23, 53, 56, 89), dy=21),
}


def timetable():
    found = []

    def put(seq, step, rank, limit, *what):
        found.append((min(step, limit), rank, len(found), seq, what))

    for seq, times in TIMES.items():
        put(seq, -1, 0, -1, "x", 1)
        group = 1
        for step, what in zip(times.get("then", ()), THEN.get(seq, ())):
            put(seq, step, 1, 12 * group - 1, *what)
            group += what == ("q", 4, 1)
        if seq % 2:
            for piece in (1, 2):
                put(seq, 12 * piece, 1, LAST_STEP, "q_from_core", piece)
        limit = LAST_STEP if seq == 3 else BEFORE_UP
        if "own" in times:
            for rank, (step, what) in enumerate(zip(times["own"], (("start",), *(("own", hops) for hops in range(1, 5))))):
                put(seq, step, 2 + (rank > 0), limit, *what)
            put(seq, times["over_x"], 2, limit, "over_x")
        limit = LAST_STEP if seq == 1 else BEFORE_UP
        if "far" in times:
            for rank, (step, what) in enumerate(zip(times["far"], (("far_start",), *(("far", hops) for hops in range(1, 5))))):
                put(seq, step, 4 + (rank > 0), limit, *what)
        if "across" in times:
            for i, place in enumerate(ACROSS_ORDER):
                step = max(times["across"][(i + 1) // 2], times["far"][abs(place)])
                put(seq, step, 6, BEFORE_UP, "across", place)
        put(seq, times["dy"], 7, LAST_STEP, "dy")
    table = {}
    for step, _, _, seq, what in sorted(found):
        table.setdefault((seq, step), []).append(what)
    return table


def forward_kernel(
    n_batch, plan, share, vec, x_in, grad_in, scored, mask,
    mats, x_out, qkv_out, att_out, lse_out, out_own, dr1_out, datt_out, act_out, du_out, h1_out, dz_out, da_out, sums,
    x_all, att, dy, dy_in, out, wide, datt, w_out, w_up, w_down, stage, act, act_t, slope, h1_t, dz, da, scales, biases, lse, masks, vecs, vec_in,
    own_sem, send_sem, mat_sem, vec_sem, seq_sem, w_sem, mask_sem, out_sem, load_sem, stage_sem, row_sem, give_sem, give_own, grad_sem,
):
    at = Place(n_batch)
    n_z, tokens = at.n_z, x_in.shape[1]
    half = at.ring // 2
    me = at.share(at.x, at.core, 0)
    sends = Sends(send_sem)
    heads = mask.shape[0]
    seqs, length = x_all.shape[:2]
    depth = share.shape[1]
    n_up = FF // D
    mine = pl.ds(at.seq * tokens, tokens)
    w, qkv = w_up, slope

    own = [
        pltpu.make_async_copy(share, mats.at[me], own_sem.at[0]),
        pltpu.make_async_copy(x_in.at[pl.ds(at.seq * seqs, seqs)], x_all.at[:, mine], own_sem.at[1]),
        pltpu.make_async_copy(dy_in.at[pl.ds(at.seq * seqs, seqs)], dy.at[:, mine], own_sem.at[2]),
    ]
    per_row = length // tokens
    grads = []
    for i in range(grad_in.shape[0]):
        there = wide.at[i // per_row, pl.ds(i % per_row * tokens, tokens)]
        grads.append(pltpu.make_async_copy(grad_in.at[i], there, grad_sem.at[i]))
    for copy in own[:2] + grads:
        copy.start()

    for unit in range(2):
        pltpu.make_async_copy(mask.at[unit], masks.at[unit], mask_sem.at[unit]).start()
    vecs[...] = vec[...]
    at.barrier()

    all_of = (0, 3, 0)
    first_of, rest_of = (0, 1, 0), (1, 3, 2)
    whole_ring = (all_of, ((0, 1, 0), (1, 3, 1)))
    rest_ring = (rest_of, ((1, 2, 1), (2, 3, 2)))

    def piece_ring(piece):
        part = (piece, piece + 1, piece)
        return (part, (part, None) if piece == 0 else (None, part))

    def part_at(index, part):
        return mats.at[index, pl.ds(part[0], part[1] - part[0])]

    def wait(index, part):
        sends.arrived(part_at(index, part), mat_sem.at[index, part[2]], at.core_peer)

    def pass_on(index, part, *peers):
        for peer in peers:
            sends.start(part_at(index, part), part_at(index, part), mat_sem.at[index, part[2]], peer, lambda: part_at(0, part))

    def lay_out(index, piece):
        rows = pl.ds(pl.multiple_of(index * depth, 32), depth)
        return pltpu.make_async_copy(mats.at[index, piece], w.at[piece, rows], w_sem.at[index, piece])

    def nothing(index):
        pass

    def round_start(x_at, ring):
        pass_on(at.share(x_at, at.core, 0), ring[0], at.next, at.prev)

    def round_step(x_at, hops, ring, then):
        for way, sign, peer in ((0, -1, at.next), (1, 1, at.prev)):
            index = at.share(x_at, at.core, sign * hops)
            part = ring[0] if hops < half else ring[1][way]
            if part:
                wait(index, part)
            onward = ring[0] if hops < half - 1 else ring[1][way] if hops == half - 1 else None
            if onward:
                pass_on(index, onward, peer)
            if hops < half:
                then(index)
        if hops == half:
            then(at.share(x_at, at.core, half))

    def vec_hop(hop, peer):
        vec_in[hop + n_z] = vecs[...]
        sends.start(vec_in.at[hop + n_z], vec_in.at[hop], vec_sem.at[hop], peer)

    def vec_take(hop):
        sends.arrived(vec_in.at[hop], vec_sem.at[hop], at.core_peer)
        vecs[...] = vecs[...] + vec_in[hop]

    def exchange(src, dst, which, seq):
        for step in (1, 2, 3):
            theirs = at.seq_at(step) * seqs + seq
            sends.start(src.at[theirs], dst.at[seq, mine], seq_sem.at[which, seq, step], at.seq_peer(step), lambda: src.at[0])

    def exchanged(dst, which, seq):
        for step in (1, 2, 3):
            theirs = pl.ds(at.seq_at(4 - step) * tokens, tokens)
            sends.arrived(dst.at[seq, theirs], seq_sem.at[which, seq, step], at.core_peer)

    is_class = [at.seq == seq for seq in range(4)]
    is_core0, is_core1 = at.core == 0, at.core == 1
    vec_hop(0, at.core_peer)
    own[0].wait()

    def q_arrived(piece, index):
        pass_on(index, piece_ring(piece)[0], at.core_peer)
        lay_out(index, piece).start()

    def q_start(seq, piece):
        index = at.share(0, 0, 0)
        if seq == 2:
            wait(index, piece_ring(piece)[0])
        round_start(0, piece_ring(piece))
        q_arrived(piece, index)

    def q_step(hops, piece):
        round_step(0, hops, piece_ring(piece), functools.partial(q_arrived, piece))

    def q_from_core(piece, first=0):
        for hops in range(first, half + 1):
            for sign in (-1, 1) if 0 < hops < half else (1,):
                index = at.share(0, 0, sign * hops)
                wait(index, piece_ring(piece)[0])
                lay_out(index, piece).start()

    def other_start(seq):
        round_start(at.x, whole_ring)
        pass_on(me, all_of, at.core_peer)

    def own_over_x(seq):
        if seq == 3:
            pass_on(me, all_of, at.x_peer)
        else:
            pass_on(me, rest_of, at.x_peer)
            pass_on(me, first_of, at.x_peer)

    def own_arrived(seq, index):
        if seq != 3:
            pass_on(index, first_of, at.x_peer)
        pass_on(index, all_of, at.core_peer)

    def far_arrived(index):
        pass_on(index, all_of, at.core_peer)

    def far_start(seq):
        index = at.share(1 - at.x, at.core, 0)
        ring = whole_ring if seq == 1 else rest_ring
        wait(index, ring[0])
        round_start(1 - at.x, ring)
        if seq == 1:
            far_arrived(index)

    def far_step(seq, hops):
        if seq == 1:
            round_step(1 - at.x, hops, whole_ring, far_arrived)
        else:
            round_step(1 - at.x, hops, rest_ring, nothing)

    def across(place):
        index = at.share(1 - at.x, at.core, place)
        wait(index, first_of)
        far_arrived(index)

    def relay(seq, what, *which):
        if what == "q":
            q_step(*which)
        elif what == "q_start":
            q_start(seq, *which)
        elif what == "q_from_core":
            q_from_core(*which)
        elif what == "start":
            other_start(seq)
        elif what == "over_x":
            own_over_x(seq)
        elif what == "own":
            round_step(at.x, *which, whole_ring, functools.partial(own_arrived, seq))
        elif what == "far_start":
            far_start(seq)
        elif what == "far":
            far_step(seq, *which)
        elif what == "across":
            across(*which)
        elif what == "x":
            exchange(x_in, x_all, 0, *which)
        else:
            for number in range(seqs):
                exchange(dy_in, dy, 1, number)

    def relay_all(seq, some):
        sends.under(is_class[seq], lambda: run([functools.partial(relay, seq, *one) for one in some]))

    def first_of_class0():
        pass_on(me, piece_ring(0)[0], at.x_peer)
        q_start(0, 0)
        sends.sent(4, 1, at.x_peer)
        exchange(x_in, x_all, 0, 0)
        for piece in (1, 2):
            pass_on(me, piece_ring(piece)[0], at.x_peer)

    def first_of_class1():
        index = at.share(0, 0, 0)
        wait(index, piece_ring(0)[0])
        lay_out(index, 0).start()
        exchange(x_in, x_all, 0, 0)

    def first_of_class2():
        exchange(x_in, x_all, 0, 0)
        q_start(2, 0)

    def first_of_class3():
        exchange(x_in, x_all, 0, 0)

    for seq, first in enumerate((first_of_class0, first_of_class1, first_of_class2, first_of_class3)):
        sends.under(is_class[seq], first)
    square = (tokens, tokens)
    diagonal = lax.broadcasted_iota(jnp.int32, square, 0) == lax.broadcasted_iota(jnp.int32, square, 1)
    for i, copy in enumerate(grads):
        copy.wait()
        column = jnp.sum(jnp.where(diagonal, scored[i : i + 1, :].astype(F32), 0.0), -1, keepdims=True)
        dy_in[i] = (wide[i // per_row, i % per_row * tokens : (i % per_row + 1) * tokens] * column).astype(BF16)
    own[2].start()
    vec_take(0)
    vec_hop(1, at.x_peer)
    for seq in (0, 2):
        relay_all(seq, FIRST[seq][:3])
    vec_take(1)
    vec_hop(2, at.y_peer)
    for seq in (0, 2):
        relay_all(seq, FIRST[seq][3:])
    sends.under(is_class[1], lambda: q_from_core(0, 1))
    sends.under(is_class[3], lambda: q_from_core(0))
    vec_take(2)
    vec_in[2 * n_z + 2] = vecs[...]
    for step in range(1, n_z):
        sends.start(vec_in.at[2 * n_z + 2], vec_in.at[2 + 2 * n_z + step], vec_sem.at[3 + step], at.z_peer(step))

    table = timetable()

    def relays(step):
        for seq in range(4):
            if (seq, step) in table:
                relay_all(seq, table[seq, step])

    def relays_in_loop(now, first, each, count):
        def turn(number):
            for step in range(first + number * each, first + (number + 1) * each):
                relays(step)

        held = {(step - first) // each for _, step in table if first <= step < first + each * count}
        dispatch(now, sorted(held), turn)

    relays(-1)
    for step in range(1, n_z):
        slot_in = 2 + 2 * n_z + step
        sends.arrived(vec_in.at[slot_in], vec_sem.at[3 + step], at.core_peer)
        vecs[...] = vecs[...] + vec_in[slot_in]
    exchanged(x_all, 0, 0)
    own[1].wait()

    grid = vecs[...]
    per = D // 128
    starts, offset = [], 0
    for size in VEC_LENGTHS:
        starts.append(offset // 128)
        offset += size
    width = D // 3
    b_q, b_v = row_of(grid, 0, per), row_of(grid, per, per)
    for piece in range(3):
        part = slice(piece * width, (piece + 1) * width)
        biases[piece, 0:1] = jnp.concatenate([b_q[:, part], jnp.zeros((1, width), F32), b_v[:, part]], 1)
    block = 256
    blocks = length // block
    outs = []

    def project(seq, piece):
        lanes = pl.ds(pl.multiple_of(piece * width, width), width)
        for i in range(blocks):
            rows = pl.ds(i * block, block)
            value = contract(x_all[seq, rows], w[piece], (1, 0)) + biases[piece, 0:1]
            for j in range(3):
                qkv[j, seq, rows, lanes] = value[:, j * width : (j + 1) * width].astype(BF16)

    lse[...] = jnp.zeros_like(lse)
    of_piece = heads // 3
    units = seqs * heads

    def fetch_mask(unit):
        slot = unit % 2
        return pltpu.make_async_copy(mask.at[unit % heads], masks.at[slot], mask_sem.at[slot])

    def one_head(unit, carry):
        seq, head = unit // heads, unit % heads
        relays_in_loop(unit, 0, 3, units)
        for piece in range(3):

            @pl.when(unit == piece * of_piece)
            def _():
                for index in range(2 * n_z):
                    lay_out(index, piece).wait()

        @pl.when(unit == heads)
        def _():
            exchanged(x_all, 0, 1)

        @pl.when(unit % of_piece == 0)
        def _():
            project(seq, head // of_piece)

        fetch_mask(unit).wait()

        attend_head(head, seq, qkv, masks.at[unit % 2], att, lse)

        @pl.when(unit + 2 < units)
        def _():
            fetch_mask(unit + 2).start()

        return carry

    lax.fori_loop(0, units, one_head, 0)
    outs.append(pltpu.make_async_copy(x_all, x_out, out_sem.at[0]))
    outs.append(pltpu.make_async_copy(qkv.at[pl.ds(0, 3)], qkv_out, out_sem.at[1]))
    outs.append(pltpu.make_async_copy(att, att_out, out_sem.at[2]))
    outs.append(pltpu.make_async_copy(lse, lse_out, out_sem.at[3]))
    for copy in outs:
        copy.start()
    relays(BEFORE_UP)

    def plane_from_core(x_at):
        for step in range(at.ring):
            wait(at.share(x_at, 1 - at.core, step), all_of)

    plane_from_core(at.core)
    loads = {"out": [], "down": []}
    for number, (name, share_at, first, begin, size) in enumerate(plan):
        if name != "up":
            target = {"out": w_out, "down": w_down}[name]
            source = mats.at[share_at, pl.ds(first // depth, size // depth)]
            loads[name].append(pltpu.make_async_copy(source, target.at[pl.ds(begin // depth, size // depth)], load_sem.at[number]))
    for copy in loads["out"]:
        copy.start()
    ups = [entry for entry in plan if entry[0] == "up"]
    pairs, group, filled = [], [], 0
    for _, share_at, first, _, size in ups:
        group.append((share_at, first, size))
        filled += size
        if filled // n_up % 16 == 0:
            pairs.append(group)
            group, filled = [], 0

    def fetch(number):
        slot = number % 2
        return [
            pltpu.make_async_copy(
                mats.at[share_at, pl.ds(first // depth, size // depth)],
                stage.at[slot, i, pl.ds(0, size // depth)],
                stage_sem.at[slot, i],
            )
            for i, (share_at, first, size) in enumerate(pairs[number])
        ]

    outs[1].wait()
    for copy in fetch(0):
        copy.start()
    line = 0
    for number, members in enumerate(pairs):
        if number + 1 < len(pairs):
            for copy in fetch(number + 1):
                copy.start()
        for copy in fetch(number):
            copy.wait()
        lines = sum(size for _, _, size in members) // n_up
        for j in range(n_up):
            pieces = []
            for i, (_, _, size) in enumerate(members):
                each = size // n_up
                low, high = j * each // 16 * 16, -(-(j + 1) * each // 16) * 16
                values = stage[number % 2, i].reshape(3 * depth, D)[low:high].astype(F32)
                pieces.append(values[j * each - low : j * each - low + each])
            w_up[j, line : line + lines] = jnp.concatenate(pieces, 0).astype(BF16)
        line += lines
    for copy in loads["out"]:
        copy.wait()

    b_o, b_2, g_1, s_1, g_2, s_2 = (row_of(grid, starts[i], per) for i in (2, 4, 5, 6, 7, 8))
    n_chunks = seqs * blocks

    def columns(i):
        return pl.ds(pl.multiple_of(i * block, block), block)

    def up_chunk(i, carry):
        relays_in_loop(i, BEFORE_UP + 1, n_up, n_chunks)
        seq, rows = i // blocks, columns(i % blocks)
        mixed = contract(att[seq, rows], w_out[...].reshape(D, D), (1, 0))
        n1, scale1 = norm_parts(x_all[seq, rows].astype(F32) + mixed + b_o)
        wide[seq, rows] = n1
        scales[seq, rows] = jnp.broadcast_to(scale1, (block, 128))
        h1_low = (n1 * g_1 + s_1).astype(BF16)
        h1_t[:, columns(i)] = h1_low.T
        for j in range(n_up):
            value = contract(h1_low, w_up[j], (1, 0)) + row_of(grid, starts[3] + j * per, per)
            phi = 0.5 * (1.0 + lax.erf(value * ROOT_HALF))
            act[j, seq, rows] = (value * phi).astype(BF16)
            slope[j, seq, rows] = (phi + value * (jnp.exp(-0.5 * value * value) * ROOT_TWO_PI_INV)).astype(BF16)
        return carry

    lax.fori_loop(0, n_chunks, up_chunk, 0)
    outs.append(pltpu.make_async_copy(h1_t, h1_out, out_sem.at[4]))
    outs[4].start()
    relays(LAST_STEP)

    sends.under(is_core0, functools.partial(plane_from_core, 1))
    for copy in loads["down"]:
        copy.start()
    for seq in range(seqs):
        exchanged(dy, 1, seq)
    own[2].wait()
    sums[...] = jnp.zeros_like(sums)
    for copy in loads["down"]:
        copy.wait()

    def rows_out(i):
        seq, rows = i // blocks, columns(i % blocks)
        pairs_of = (
            (wide.at[seq, rows], dr1_out.at[seq, rows]),
            (datt.at[seq, rows], datt_out.at[seq, rows]),
            (act_t.at[:, columns(i)], act_out.at[:, columns(i)]),
            (slope.at[:, seq, rows], du_out.at[:, seq, rows]),
            (dz.at[seq, rows], dz_out.at[seq, rows]),
            (da.at[seq, rows], da_out.at[seq, rows]),
        )
        return [pltpu.make_async_copy(src, dst, row_sem.at[k, i]) for k, (src, dst) in enumerate(pairs_of)]

    holders = block // tokens

    def give(i, e):
        seq = i // blocks
        holder = i % blocks * holders + e
        src = out.at[seq, pl.ds(pl.multiple_of(holder * tokens, tokens), tokens)]
        dst = out_own.at[at.seq * seqs + seq]
        step = (holder - at.seq + 4) % 4
        remote = pltpu.make_async_remote_copy(
            src_ref=src,
            dst_ref=dst,
            send_sem=give_sem.at[0, i, e],
            recv_sem=give_sem.at[1, seq, step],
            device_id={"seq": holder},
            device_id_type=MESH,
        )
        return holder != at.seq, remote, pltpu.make_async_copy(src, dst, give_own.at[seq])

    def down_chunk(i, carry):
        seq, rows = i // blocks, columns(i % blocks)
        n1 = wide[seq, rows]
        scale1 = scales[seq, rows][:, 0:1]
        total = n1 * g_1 + s_1 + b_2
        for j in range(n_up):
            value = act[j, seq, rows]
            act_t[pl.ds(j * D, D), columns(i)] = value.T
            total = total + contract(value, w_down[pl.ds(j * D // depth, D // depth)].reshape(D, D), (1, 0))
        n2, scale2 = norm_parts(total)
        out[seq, rows] = (n2 * g_2 + s_2).astype(BF16)
        for e in range(holders):
            away, remote, here = give(i, e)
            pl.when(away)(remote.start)
            pl.when(jnp.logical_not(away))(here.start)
        d = dy[seq, rows].astype(F32)
        sums[0:1] += jnp.sum(d * n2, 0, keepdims=True)
        sums[1:2] += jnp.sum(d, 0, keepdims=True)
        dr2 = norm_back(d, n2, scale2, g_2)
        dz_low = dr2.astype(BF16)
        dz[seq, rows] = dz_low
        dh1 = dr2
        for j in range(n_up):
            grad = contract(dz_low, w_down[pl.ds(j * D // depth, D // depth)].reshape(D, D), (1, 1))
            du = (grad * slope[j, seq, rows].astype(F32)).astype(BF16)
            slope[j, seq, rows] = du
            dh1 = dh1 + contract(du, w_up[j], (1, 1))
        sums[2:3] += jnp.sum(dh1 * n1, 0, keepdims=True)
        sums[3:4] += jnp.sum(dh1, 0, keepdims=True)
        d1 = norm_back(dh1, n1, scale1, g_1)
        wide[seq, rows] = d1
        da_low = d1.astype(BF16)
        da[seq, rows] = da_low
        datt[seq, rows] = contract(da_low, w_out[...].reshape(D, D), (1, 1)).astype(BF16)
        for copy in rows_out(i):
            copy.start()
        return carry

    lax.fori_loop(0, n_chunks, down_chunk, 0)

    for i in range(n_chunks):
        for copy in rows_out(i):
            copy.wait()
        for e in range(holders):
            away, remote, here = give(i, e)
            pl.when(away)(remote.wait_send)
            pl.when(jnp.logical_not(away))(here.wait)
    for seq in range(seqs):
        for step in (1, 2, 3):
            dst = out_own.at[at.seq_at(4 - step) * seqs + seq]
            sends.arrived(dst, give_sem.at[1, seq, step], at.core_peer)
    for copy in outs[:1] + outs[2:]:
        copy.wait()
    sends.drain(at.core_peer)


def forward(n_batch, share, vec, x_in, grad_in, scored, mask):
    rows = share.shape[0]
    depth = rows // 3
    shares = 4 * n_batch
    n_z = n_batch // 2
    n_up = FF // D
    seqs, length = x_in.shape[0] // 4, 4 * x_in.shape[1]
    tokens = seqs * length
    plan = []
    for number in range(shares):
        for name, _, at, begin, size in segments(number, rows):
            if name != "qkv":
                plan.append((name, number, at, begin, size))
    whole, low, gelu = (seqs, length, D), (D, tokens), (n_up, seqs, length, D)
    share = share.reshape(3, depth, D)
    outs = [
        ((shares,) + share.shape, BF16),
        (whole, BF16),
        ((3,) + whole, BF16),
        (whole, BF16),
        ((seqs, length, 128), F32),
        (x_in.shape, BF16),
        (whole, F32),
        (whole, BF16),
        ((FF, tokens), BF16),
        (gelu, BF16),
        (low, BF16),
        (whole, BF16),
        (whole, BF16),
        ((8, D), F32),
    ]
    vmem = [
        (whole, BF16),
        (whole, BF16),
        (whole, BF16),
        (x_in.shape, BF16),
        (whole, BF16),
        (whole, F32),
        (whole, BF16),
        ((D // depth, depth, D), BF16),
        ((n_up, D, D), BF16),
        ((FF // depth, depth, D), BF16),
        ((2, 2, 3, depth, D), BF16),
        (gelu, BF16),
        ((FF, tokens), BF16),
        (gelu, BF16),
        (low, BF16),
        (whole, BF16),
        (whole, BF16),
        ((seqs, length, 128), F32),
        ((3, 8, D), F32),
        ((seqs, length, 128), F32),
        ((2, length, length), jnp.int32),
        (vec.shape, F32),
        ((3 * n_z + 3,) + vec.shape, F32),
    ]
    blocks = tokens // 256
    sems = [(3,), (400,), (shares, 3), (n_z + 3,), (2, seqs, 4), (2 * n_z, 3), (2,), (5,), (len(plan),), (2, 2), (6, blocks), (2, blocks, 4), (seqs,), (x_in.shape[0],)]
    return pl.pallas_call(
        functools.partial(forward_kernel, n_batch, plan),
        out_shape=[jax.ShapeDtypeStruct(shape, dtype) for shape, dtype in outs],
        in_specs=[ANY, VMEM, ANY, ANY, VMEM, ANY],
        out_specs=[ANY] * 13 + [VMEM],
        scratch_shapes=[pltpu.VMEM(shape, dtype) for shape, dtype in vmem]
        + [pltpu.SemaphoreType.DMA(shape) for shape in sems],
        compiler_params=pltpu.CompilerParams(
            collective_id=0, has_side_effects=True, vmem_limit_bytes=60 * MIB
        ),
        name="forward",
    )(share, vec, x_in, grad_in, scored, mask)


PLACES = (4, 3, -3, 2, -2, 1, -1, 0)
REDUCE_TIMES = {
    0: dict(over_x=(-2, -2, 0, 14, 8, 13, 8, 17), late=((5, 13, 16, 26, 28, 28), (16, 19, 22, 24, 28, 28), (3, 3, 5, 27, 28, 28))),
    1: dict(kind0=(9, 20, 27, 28, 28), kind1=(0, 5, 9, 15, 17, 22)),
    2: dict(kind0=(5, 9, 25, 27, 28), late=((12, 14, 16, 17, 21, 28), (16, 18, 21, 24, 25, 25), (16, 16, 25, 26, 27, 28))),
    3: dict(over_x=(4, 7, 7, 17, 9, 12, 11, 17), kind1=(0, 6, 10, 19, 27, 27)),
}


def reduction_table():
    found = []
    ring = (("begin",), ("hop", 1), ("hop", 2), ("hop", 3), ("end",), ("last",))
    for seq, times in REDUCE_TIMES.items():
        for i, step in enumerate(times.get("over_x", ())):
            found.append((step, 0, i, seq, ("x", PLACES[i])))
        for kind in (0, 1):
            for i, step in enumerate(times.get(f"kind{kind}", ())):
                found.append((step, 1 + kind, i, seq, ("ring", kind, None) + ring[i]))
        for piece in range(3):
            for i, step in enumerate(times.get("late", ((), (), ()))[piece]):
                found.append((max(step, 8 * (piece + 1)), 3 + piece, i, seq, ("ring", 1, piece) + ring[i]))
    table = {}
    for step, _, _, seq, what in sorted(found):
        table.setdefault((seq, step), []).append(what)
    return table


def finish_kernel(
    n_batch, mask, qkv_in, att_in, datt_in, lse_in, x_in, mats, dr1_in, act_in, du_in, h1_in, dz_in, da_in, sums,
    share, vec_out, dx_own,
    qkv, att, datt, lse, w, wide, dqkv, dx, turned, act_t, masks, probs, dscore, grads, from_core, x_a, ring_in, x_b, vec_in,
    in_sem, mask_sem, act_sem, du_sem, own_sem, send_sem, core_sem, a_sem, ring_sem, b_sem, vec_sem, seq_sem,
):
    at = Place(n_batch)
    rows = grads.shape[2]
    heads = mask.shape[0]
    n_z, tokens = at.n_z, dx_own.shape[1]
    seqs, length = att.shape[:2]
    depth = rows // 3
    n_up = FF // D
    half = at.ring // 2
    sends = Sends(send_sem)
    mine = pl.ds(at.seq * tokens, tokens)
    dz, da, x = dqkv.at[2], dx, dx

    ins = [
        pltpu.make_async_copy(src, dst, in_sem.at[i])
        for i, (src, dst) in enumerate(
            ((dz_in, dz), (att_in, att), (h1_in, turned), (da_in, da), (qkv_in, qkv), (datt_in, datt), (lse_in, lse))
        )
    ]

    def fetch_act(j):
        return pltpu.make_async_copy(act_in.at[pl.ds(j * D, D)], act_t.at[j % 2], act_sem.at[j % 2])

    def fetch_du(j):
        return pltpu.make_async_copy(du_in.at[j], dqkv.at[j % 2], du_sem.at[j % 2])

    def fetch_mask(head):
        slot = head % 2
        return pltpu.make_async_copy(mask.at[head], masks.at[slot], mask_sem.at[slot])

    ins[0].start()
    down_order = [*range(1, n_up), 0]
    fetch_act(down_order[0]).start()
    fetch_act(down_order[1]).start()
    for copy in ins[1:]:
        copy.start()
    fetch_du(0).start()
    fetch_du(1).start()
    fetch_mask(0).start()
    fetch_mask(1).start()
    loads = []
    for index in range(n_batch):
        target = w.at[:, pl.ds(index * depth, depth)]
        loads.append(pltpu.make_async_copy(mats.at[index], target, in_sem.at[9 + index]))
        loads[-1].start()
    at.barrier()

    is_class = [at.seq == seq for seq in range(4)]
    on_core = (at.core == 0, at.core == 1)

    def plane_of(core, kind):
        return (2 - core, 3 * core)[kind]

    order = [half] + [sign * hops for hops in range(half - 1, 0, -1) for sign in (1, -1)] + [0]

    def part_rows(part):
        return pl.ds(part[0] * depth, (part[1] - part[0]) * depth)

    def to_core(core, kind, part=(0, 3)):
        lines = part_rows(part)
        for step in order:
            b = at.around(step)
            source = grads.at[plane_of(1 - core, kind), b, lines]
            sends.start(source, from_core.at[kind, b, lines], core_sem.at[kind, b, part[0]], at.core_peer, lambda: from_core.at[0, 0, lines])

    def is_own(seq, kind):
        return (seq // 2 == seq % 2) == (kind == 1)

    def ring_of(own, kind, piece):
        if piece is not None:
            part = (piece, piece + 1)
            return part, (part, None) if piece == 0 else (None, part)
        if kind == 1 or own:
            return (0, 3), ((0, 1), (1, 3))
        return None, (None, None)

    def add(seq, kind, b, part, *others, into=None):
        low, high = part
        terms = [grads.at[plane_of(seq % 2, kind), b], *others]
        if kind == 0 and is_own(seq, 0):
            terms.append(x_a.at[b])
        lines = part_rows(part)
        target = from_core.at[kind, b]
        if into is not None:
            into[lines] = from_core[kind, b, lines].astype(F32)
            target = into
        add_rows(target, (low * depth, (high - low) * depth), *[(ref, low * depth) for ref in terms])

    def ready(seq, kind, b, piece):
        part = (0, 3) if piece is None else (piece, piece + 1)
        here = from_core.at[kind, b, part_rows(part)]
        if not (kind == 0 and not is_own(seq, 0)):
            sends.arrived(here, core_sem.at[kind, b, part[0]], at.core_peer)
        if kind == 0 and is_own(seq, 0):
            sends.arrived(x_a.at[b], a_sem.at[b], at.core_peer)

    def ring_send(kind, b, way, hops, part):
        peer = (at.next, at.prev)[way]
        lines = part_rows(part)
        sends.start(from_core.at[kind, b, lines], ring_in.at[kind, way, hops, lines], ring_sem.at[kind, way, hops, part[0]], peer, lambda: ring_in.at[0, 0, 0, lines])

    def ring_wait(kind, way, hops, part):
        sends.arrived(ring_in.at[kind, way, hops, part_rows(part)], ring_sem.at[kind, way, hops, part[0]], at.core_peer)
        return ring_in.at[kind, way, hops]

    def ring_step(seq, kind, piece, what, hops=0):
        own = is_own(seq, kind)
        whole, opposite = ring_of(own, kind, piece)
        if what == "begin":
            b = at.around(half)
            ready(seq, kind, b, piece)
            for way, part in enumerate(opposite):
                if part:
                    add(seq, kind, b, part)
                    ring_send(kind, b, way, 0, part)
        elif what == "hop":
            for way, b in enumerate((at.around(half - hops), at.around(hops - half))):
                ready(seq, kind, b, piece)
                if hops > 1:
                    add(seq, kind, b, whole, ring_wait(kind, way, hops - 1, whole))
                else:
                    part = opposite[way]
                    if part:
                        add(seq, kind, b, part, ring_wait(kind, way, 0, part))
                    for low, high in ((whole[0], part[0]), (part[1], whole[1])) if part else (whole,):
                        if low < high:
                            add(seq, kind, b, (low, high))
                ring_send(kind, b, way, hops, whole)
        elif what == "end":
            b = at.batch
            ready(seq, kind, b, piece)
            others = [ring_wait(kind, way, half - 1, whole) for way in range(2)]
            add(seq, kind, b, whole, *others, into=share if own else None)
            if not own:
                lines = part_rows(whole)
                sends.start(from_core.at[kind, b, lines], x_b.at[lines], b_sem.at[whole[0]], at.x_peer, lambda: x_b.at[lines])
        elif own:
            far_part = ring_of(False, kind, piece)[0]
            sends.arrived(x_b.at[part_rows(far_part)], b_sem.at[far_part[0]], at.core_peer)
            add_rows(share, (far_part[0] * depth, (far_part[1] - far_part[0]) * depth), (x_b, far_part[0] * depth))

    def over_x(seq, step):
        b = at.around(step)
        here = from_core.at[0, b]
        sends.arrived(here, core_sem.at[0, b, 0], at.core_peer)
        add(seq, 0, b, (0, 3))
        sends.start(here, x_a.at[b], a_sem.at[b], at.x_peer, lambda: x_a.at[0])

    table = reduction_table()

    def reduce_at(step):
        for seq in range(4):
            some = table.get((seq, step))
            if some:
                steps = [functools.partial(over_x if what[0] == "x" else ring_step, seq, *what[1:]) for what in some]
                sends.under(is_class[seq], functools.partial(run, steps))

    base_down, base_up, base_out = 3 * D + D + FF, 3 * D + D, 3 * D

    def put(row, values):
        done = 0
        while done < values.shape[0]:
            number, first = (row + done) // rows, (row + done) % rows
            size = min(values.shape[0] - done, rows - first)
            grads[number // n_batch, number % n_batch, first : first + size] = values[done : done + size]
            done += size

    starts, offset = [], 0
    for size in VEC_LENGTHS:
        starts.append(offset // 128)
        offset += size
    per = D // 128

    def put_vec(first, value):
        for i in range(value.shape[1] // 128):
            vec_out[first + i : first + i + 1, :] = value[0:1, i * 128 : (i + 1) * 128]

    ones = jnp.ones((16, seqs * length), BF16)
    block = D // 2

    def flat(values):
        return values.reshape(seqs * length, D)

    vec_out[...] = jnp.zeros_like(vec_out)
    ins[0].wait()
    for number, j in enumerate(down_order):
        fetch_act(j).wait()
        for i in range(D // block):
            put(base_down + j * D + i * block, contract(act_t[j % 2, i * block : (i + 1) * block], flat(dz[...]), (1, 0)).astype(BF16))
        if number + 2 < n_up:
            fetch_act(down_order[number + 2]).start()
        if number == n_up - 2:
            sends.under(on_core[0], functools.partial(to_core, 0, 1))
    put_vec(starts[4], contract(ones, flat(dz[...]), (1, 0)))
    reduce_at(-3)
    ins[2].wait()
    ups = []
    for number in range(4 * n_batch):
        ups += [(number, at_row, begin, size) for name, _, at_row, begin, size in segments(number, rows) if name == "up"]
    middle = D // 2
    for high in (1, 0):
        for pair in range(n_up // 2):
            for k in range(2):
                j = pair * 2 + k
                fetch_du(j).wait()
                wide[k, 0:middle] = contract(turned[high * middle : (high + 1) * middle], flat(dqkv[j % 2]), (1, 0))
                if high:
                    put_vec(starts[3] + j * per, contract(ones, flat(dqkv[j % 2]), (1, 0)))
                if not (high == 0 and pair == n_up // 2 - 1):
                    fetch_du((j + 2) % n_up).start()
            for number, at_row, begin, size in ups:
                count, low = size // n_up, begin // n_up - high * middle
                if 0 <= low < middle:
                    both = jnp.concatenate([wide[k, low : low + count] for k in range(2)], 0).astype(BF16)
                    at_row += pair * 2 * count
                    grads[number // n_batch, number % n_batch, at_row : at_row + 2 * count] = both
        if high:
            sends.under(on_core[1], functools.partial(to_core, 1, 0))
            reduce_at(-2)
    ins[1].wait()
    ins[3].wait()
    for seq in range(seqs):
        turned[:, seq * length : (seq + 1) * length] = att[seq].T
    for i in range(D // block):
        put(base_out + i * block, contract(turned[i * block : (i + 1) * block], flat(da[...]), (1, 0)).astype(BF16))
    sends.under(on_core[0], functools.partial(to_core, 0, 0))
    put_vec(starts[2], contract(ones, flat(da[...]), (1, 0)))
    for i, line in enumerate((starts[7], starts[8], starts[5], starts[6])):
        put_vec(line, sums[i : i + 1])

    dr1_copy = pltpu.make_async_copy(dr1_in, wide, in_sem.at[8])
    dr1_copy.start()
    x_copy = pltpu.make_async_copy(x_in, x, in_sem.at[7])
    x_copy.start()
    for copy in ins[4:]:
        copy.wait()
    x_copy.wait()
    for seq in range(seqs):
        turned[:, seq * length : (seq + 1) * length] = x[seq].T

    reduce_at(-1)

    units = heads * seqs
    of_piece = heads // 3
    width = D // 3
    lines = 4 * depth

    def qkv_gradient(piece):
        lanes = slice(piece * width, (piece + 1) * width)
        for j in range(3):
            right = dqkv[j, :, :, lanes].reshape(seqs * length, width)
            for i in range(D // lines):
                total = contract(turned[i * lines : (i + 1) * lines], right, (1, 0)).astype(BF16)
                for k in range(4):
                    grads[0, 4 * i + k, piece * depth : (piece + 1) * depth, j * width : (j + 1) * width] = total[k * depth : (k + 1) * depth]
        sends.under(on_core[1], functools.partial(to_core, 1, 1, (piece, piece + 1)))

    def one_head(head, carry):
        fetch_mask(head).wait()

        def one_seq(seq, carry):
            dispatch(head * seqs + seq, [step for step in range(units) if any((some, step) in table for some in range(4))], reduce_at)
            head_backward(head, seq, qkv, masks.at[head % 2], att, datt, lse, probs, dscore, dqkv)
            return carry

        lax.fori_loop(0, seqs, one_seq, 0)

        @pl.when(head + 2 < heads)
        def _():
            fetch_mask(head + 2).start()

        for piece in range(3):
            pl.when(head == (piece + 1) * of_piece - 1)(functools.partial(qkv_gradient, piece))
        return carry

    lax.fori_loop(0, heads, one_head, 0)
    for j in (0, 2):
        put_vec(starts[j // 2], contract(ones, flat(dqkv[j]), (1, 0)))

    def vec_hop(hop, peer):
        vec_in[hop + n_z] = vec_out[...]
        sends.start(vec_in.at[hop + n_z], vec_in.at[hop], vec_sem.at[hop], peer)

    def vec_take(hop):
        sends.arrived(vec_in.at[hop], vec_sem.at[hop], at.core_peer)
        vec_out[...] = vec_out[...] + vec_in[hop]

    vec_hop(0, at.core_peer)

    dr1_copy.wait()
    for copy in loads:
        copy.wait()
    for number, step in enumerate((1, 2, 3, 0)):
        reduce_at(units + number)
        theirs = pl.ds(pl.multiple_of(at.seq_at(step) * tokens, tokens), tokens)
        for seq in range(seqs):
            total = wide[seq, theirs]
            for j in range(3):
                for piece in range(3):
                    left = dqkv[j, seq, theirs, piece * width : (piece + 1) * width]
                    total = total + contract(left, w[piece, :, j * width : (j + 1) * width], (1, 1))
            dx[seq, theirs] = total.astype(BF16)
        there = dx_own.at[pl.ds(at.seq * seqs, seqs)]
        if step:
            sends.start(dx.at[:, theirs], there, seq_sem.at[step], at.seq_peer(step), lambda: dx.at[:, pl.ds(0, tokens)])
        if number == 1:
            vec_take(0)
            vec_hop(1, at.x_peer)
    own_dx = pltpu.make_async_copy(dx.at[:, mine], dx_own.at[pl.ds(at.seq * seqs, seqs)], own_sem.at[0])
    own_dx.start()
    vec_take(1)
    vec_hop(2, at.y_peer)
    reduce_at(units + 4)
    vec_take(2)
    vec_in[2 * n_z + 2] = vec_out[...]
    for step in range(1, n_z):
        sends.start(vec_in.at[2 * n_z + 2], vec_in.at[2 + 2 * n_z + step], vec_sem.at[3 + step], at.z_peer(step))
    reduce_at(units + 5)
    for step in range(1, n_z):
        slot_in = 2 + 2 * n_z + step
        sends.arrived(vec_in.at[slot_in], vec_sem.at[3 + step], at.core_peer)
        vec_out[...] = vec_out[...] + vec_in[slot_in]
    for step in (1, 2, 3):
        theirs = pl.ds(at.seq_at(4 - step) * seqs, seqs)
        sends.arrived(dx_own.at[theirs], seq_sem.at[step], at.core_peer)
    own_dx.wait()
    sends.drain(at.core_peer)


def finish(n_batch, mask, qkv, att, datt, lse, x, mats, dr1, act_t, du, h1_t, dz, da, sums):
    _, _, depth, _ = mats.shape
    rows = 3 * depth
    length = mask.shape[1]
    n_z = n_batch // 2
    seqs = att.shape[0]
    whole = (att.shape, BF16)
    turned = (D, seqs * length)
    vec = (sum(VEC_LENGTHS) // 128, 128)
    vmem = [
        (qkv.shape, BF16),
        whole,
        whole,
        (lse.shape, F32),
        ((3, D, D), BF16),
        (att.shape, F32),
        (qkv.shape, BF16),
        whole,
        (turned, BF16),
        ((2,) + turned, BF16),
        ((2, length, length), jnp.int32),
        ((length, length), BF16),
        ((length, length), BF16),
        ((4, n_batch, rows, D), BF16),
        ((2, n_batch, rows, D), BF16),
        ((n_batch, rows, D), BF16),
        ((2, 2, n_z, rows, D), BF16),
        ((rows, D), BF16),
        ((3 * n_z + 3,) + vec, F32),
    ]
    sems = [(9 + n_batch,), (2,), (2,), (2,), (1,), (400,), (2, n_batch, 3), (n_batch,), (2, 2, n_z, 3), (3,), (n_z + 3,), (4,)]
    return pl.pallas_call(
        functools.partial(finish_kernel, n_batch),
        out_shape=(
            jax.ShapeDtypeStruct((rows, D), F32),
            jax.ShapeDtypeStruct(vec, F32),
            jax.ShapeDtypeStruct((seqs * 4, length // 4, D), BF16),
        ),
        in_specs=[ANY] * 13 + [VMEM],
        out_specs=[VMEM, VMEM, ANY],
        scratch_shapes=[pltpu.VMEM(shape, dtype) for shape, dtype in vmem]
        + [pltpu.SemaphoreType.DMA(shape) for shape in sems],
        compiler_params=pltpu.CompilerParams(
            collective_id=1, has_side_effects=True, vmem_limit_bytes=62 * MIB
        ),
        name="finish",
    )(mask, qkv, att, datt, lse, x, mats, dr1, act_t, du, h1_t, dz, da, sums)


def attention(qkv, mask):
    heads = mask.shape[0]
    q, k, v = (part.reshape(part.shape[:2] + (heads, D // heads)) for part in qkv)
    scores = jnp.einsum("bqhd,bkhd->bhqk", q, k, preferred_element_type=F32) / math.sqrt(D // heads)
    scores = jnp.where(mask > 0, scores, NEG_FILL)
    largest = jnp.max(scores, -1, keepdims=True)
    expo = jnp.exp(scores - largest)
    total = jnp.sum(expo, -1, keepdims=True)
    probs = (expo / total).astype(BF16)
    mixed = jnp.einsum("bhqk,bkhd->bqhd", probs, v, preferred_element_type=F32)
    return mixed.astype(BF16).reshape(qkv.shape[1:])


def middle_plain(mats, vecs, x, att, dy):
    pieces, offset = [], 0
    for size in VEC_LENGTHS:
        pieces.append(vecs.reshape(-1)[offset : offset + size])
        offset += size
    _, _, b_o, b_1, b_2, g_1, s_1, g_2, s_2 = pieces
    w_out, w_down = (take_matrix(mats, name)[0] for name in ("out", "down"))
    w_up = take_matrix(mats, "up").swapaxes(0, 1).reshape(D, FF)
    r1 = x.astype(F32) + jnp.dot(att, w_out, preferred_element_type=F32) + b_o
    h1 = layer_norm(r1, g_1, s_1)
    h1_low = h1.astype(BF16)
    up = jnp.dot(h1_low, w_up, preferred_element_type=F32) + b_1
    act = gelu_exact(up).astype(BF16)
    r2 = h1 + jnp.dot(act, w_down, preferred_element_type=F32) + b_2
    out = layer_norm(r2, g_2, s_2).astype(BF16)
    _, norm_two_back = jax.vjp(layer_norm, r2, g_2, s_2)
    dr2, dg_2, ds_2 = norm_two_back(dy.astype(F32))
    dz = dr2.astype(BF16)
    _, gelu_back = jax.vjp(gelu_exact, up)
    du = gelu_back(contract_cols(dz, w_down))[0].astype(BF16)
    dh1 = dr2 + contract_cols(du, w_up)
    _, norm_one_back = jax.vjp(layer_norm, r1, g_1, s_1)
    dr1, dg_1, ds_1 = norm_one_back(dh1)
    da = dr1.astype(BF16)
    datt = contract_cols(da, w_out).astype(BF16)
    mats_grad = {
        "out": contract_rows(att, da)[None],
        "up": contract_rows(h1_low, du).reshape(D, FF // D, D).swapaxes(0, 1),
        "down": contract_rows(act, dz)[None],
    }
    sums = [jnp.sum(member.astype(F32), 0) for member in (da, du, dz)]
    return out, dr1, datt, mats_grad, jnp.concatenate(sums + [dg_1, ds_1, dg_2, ds_2])


def finish_plain(mask, qkv, datt, x, w_qkv, dr1):
    heads = mask.shape[0]
    seqs, length, _ = x.shape
    split = (seqs, length, heads, D // heads)
    q, k, v = (part.reshape(split) for part in qkv)
    g = datt.reshape(split)
    scale = 1.0 / math.sqrt(D // heads)
    scores = jnp.einsum("bqhd,bkhd->bhqk", q, k, preferred_element_type=F32) * scale
    probs = jax.nn.softmax(jnp.where(mask > 0, scores, NEG_FILL), -1)
    dprobs = jnp.einsum("bqhd,bkhd->bhqk", g, v, preferred_element_type=F32)
    inner = jnp.sum(probs * dprobs, -1, keepdims=True)
    dscore = (probs * (dprobs - inner)).astype(BF16)
    dq = jnp.einsum("bhqk,bkhd->bqhd", dscore, k, preferred_element_type=F32) * scale
    dk = jnp.einsum("bhqk,bqhd->bkhd", dscore, q, preferred_element_type=F32) * scale
    dv = jnp.einsum("bhqk,bqhd->bkhd", probs.astype(BF16), g, preferred_element_type=F32)
    dqkv = jnp.stack([dq, dk, dv]).astype(BF16).reshape(3, seqs * length, D)
    dw = jnp.stack([contract_rows(x.reshape(-1, D), part) for part in dqkv])
    dx = dr1 + sum(contract_cols(dqkv[j], w_qkv[j]) for j in range(3))
    db = [jnp.sum(dqkv[j].astype(F32), 0) for j in (0, 2)]
    return dw, dx.astype(BF16).reshape(x.shape), jnp.concatenate(db)


def local(
    n_batch,
    inputs,
    out_grad,
    out_mask,
    attn_mask,
    mat_param,
    mat_first,
    mat_second,
    vec_param,
    vec_first,
    vec_second,
):
    shares = 4 * n_batch
    share_rows = mat_param.shape[0] // D
    vec_len = vec_param.shape[0]
    me = lax.axis_index("seq") * n_batch + lax.axis_index("batch")

    share = rearrange(me, shares, mat_param.reshape(share_rows, D).astype(BF16), by_columns)
    vec_share = lax.dynamic_update_slice(
        jnp.zeros((shares * vec_len,), F32), vec_param.astype(BF16).astype(F32), (me * vec_len,)
    ).reshape(-1, 128)
    if share_rows % 96 == 0 and share_rows * n_batch == 3 * D:
        mats, x_all, qkv, attended, lse, outputs, *middle = forward(
            n_batch, share, vec_share, inputs, out_grad, out_mask, attn_mask
        )
        dr1, datt, *middle = middle
        mat_grad, vec_sum, dx = finish(n_batch, attn_mask, qkv, attended, datt, lse, x_all, mats, dr1, *middle)
        vec_grad = lax.dynamic_slice_in_dim(vec_sum.reshape(-1), me * vec_len, vec_len)
    else:
        mats = lax.all_gather(share, ("seq", "batch"))
        vecs = lax.psum(vec_share, ("seq", "batch")).reshape(-1)
        dy_low = (out_grad * out_mask[..., None].astype(F32)).astype(BF16)
        x_all, dy_all = (
            lax.all_to_all(member, "seq", 0, 1, tiled=True) for member in (inputs, dy_low)
        )
        whole = x_all.shape
        flat = (whole[0] * whole[1], D)
        w_qkv = regroup(take_matrix(mats, "qkv"))
        proj = jnp.stack([jnp.dot(x_all.reshape(flat), part, preferred_element_type=F32) for part in w_qkv])
        proj = proj + jnp.stack([vecs[:D], jnp.zeros((D,), F32), vecs[D : 2 * D]])[:, None]
        qkv = proj.astype(BF16).reshape((3,) + whole)
        attended = attention(qkv, attn_mask).reshape(flat)
        out_all, dr1, datt, mats_grad, grad_vecs = middle_plain(
            mats, vecs, x_all.reshape(flat), attended, dy_all.reshape(flat)
        )
        mats_grad["qkv"], dx_all, db = finish_plain(attn_mask, qkv, datt, x_all, w_qkv, dr1)
        mats_grad["qkv"] = regroup(mats_grad["qkv"])
        grads = to_shares({name: part.astype(BF16) for name, part in mats_grad.items()}, shares)
        mat_grad = lax.psum_scatter(grads.astype(F32), ("seq", "batch"))
        vec_grad = lax.psum_scatter(jnp.concatenate([db, grad_vecs]), ("seq", "batch"), tiled=True)
        outputs, dx = (
            lax.all_to_all(member, "seq", 1, 0, tiled=True) for member in (out_all.reshape(whole), dx_all)
        )
    mat_grad = rearrange(me, shares, mat_grad, by_rows).reshape(-1)
    return (
        outputs,
        dx.astype(F32),
        *adam_step(mat_param, mat_first, mat_second, mat_grad, MATS_RATE),
        *adam_step(vec_param, vec_first, vec_second, vec_grad, VECS_RATE),
    )


def solution(mesh):
    flat = P(("seq", "batch"))
    tokens = P("batch", "seq", None)
    return jax.shard_map(
        functools.partial(local, mesh.shape["batch"]),
        mesh=mesh,
        in_specs=(tokens, tokens, P("batch", "seq"), P()) + (flat,) * 6,
        out_specs=(tokens, tokens) + (flat,) * 6,
        check_vma=False,
    )
```

time: 1080 us -> 274 us (0.25)
  waiting for transfers between devices: 507 us -> 0 us
  Pallas kernels: 0 us -> 254 us
  local copies, waits for them, and re-layouts: 219 us -> 6.34 us
  matrix products: 163 us -> 0 us
  blocking collectives: 84.2 us -> 0 us
  other arithmetic: 76.6 us -> 8.83 us
  between operations: 15.2 us -> 1.03 us
    unnamed x9 -> x0, waiting for transfers between devices: 383 us -> none
    pallas_call x0 -> x2, Pallas kernels: none -> 254 us  [the longest x1 137 us: forward(): pl.pallas_call(functools.partial(forward_kernel, n_batch, plan), out_shap...]
    dot_general x26 -> x0, matrix products: 163 us -> none  [the longest x2 23.2 us: contract_cols(): lax.dot_general(operand_one, operand_two, (((1,), (1,)), ((), ())), prefe...]
    unnamed x115 -> x17, local copies, waits for them, and re-layouts: 127 us -> 1.19 us
    all_gather x3 -> x0, waiting for transfers between devices: 124 us -> none  [the longest x1 64.8 us: local(): lax.all_gather(mat_param.astype(jnp.bfloat16), ('seq', 'batch'), axis=0,...]
    unnamed x2 -> x0, blocking collectives: 84.2 us -> none
    slice x11 -> x0, local copies, waits for them, and re-layouts: 46.6 us -> none  [the longest x2 18.2 us: unpack_mats(): flat[third:].reshape(FF, D)]
    concatenate x2 -> x0, other arithmetic: 26.5 us -> none  [the longest x1 26.5 us: local(): jnp.concatenate([grad_w_qkv.reshape(-1), grad_w_out.reshape(-1), grad_w_u...]
  transfers between devices with their start and end apart: 6 -> 0, of which waited for: 5 -> 0; matrix products, arithmetic and copies ran while one was open for 15% -> 0% of each run, Pallas kernels for 0% -> 0%
where the time goes in v1:
time: 274 us; the launch traced here: 271 us
  Pallas kernels  254 us (93%)
  other arithmetic  8.83 us (3%)
  local copies, waits for them, and re-layouts  6.34 us (2%)
    pallas_call x1, Pallas kernels, forward(): pl.pallas_call(functools.partial(forward_kernel, n_batch, plan), out_shap...  137 us
    pallas_call x1, Pallas kernels, finish(): pl.pallas_call(functools.partial(finish_kernel, n_batch), out_shape=(jax....  117 us

profile of v1, /device:TPU:0, one launch (start us, length us, event | category | flops | bytes accessed | tf_op | source)
XLA Modules:
  0.0 270.5 jit_solution(15840152736933144136)
XLA Ops:
  0.7 0.8 convert_dynamic-update-slice_fusion
  1.5 0.0 copy-start.4
  1.5 1.2 convert_element_type.58
  2.7 0.4 convert_element_type.59
  3.1 0.0 copy-done.4
  3.1 1.0 conditional.2
  3.1 0.2 reshape.74
  3.3 0.3 copy.24
  3.6 0.5 reshape.75
  4.1 136.9 %forward.1 = (bf16[32,3,96,768]{3,2,1,0:T(8,128)(2,1)}, bf16[2,512,768]{2,1,0:T(8,128)(2,1)}, bf16[3,2,512,768]{3,2,1,0:T(8,128)(2,1)}, bf16[2,512,768]{2,1,0:T(...) custom-call(bf16[3,96,768]{2,1,0:T(8,128)(2,1)S(1)} %get-tuple-eleme, ...), custom_call_target="tpu_custom_call" | custom-call | tf_op jit(solution)/shard_map/forward/pallas_call | solution.py:970
  141.0 0.0 copy-start.5
  141.1 0.0 copy-start.6
  141.1 0.0 copy-start.7
  141.1 117.3 %finish.1 = (f32[288,768]{1,0:T(8,128)S(1)}, f32[72,128]{1,0:T(8,128)}, bf16[8,128,768]{2,1,0:T(8,128)(2,1)}) custom-call(s32[12,512,512]{2,1,0:T(8,128)} %mask.3, bf16[3,2,512,768]{3,2,1,0:T(8,128)(2,1)} %get-tuple-element.58.qkv_in, bf16[2,512,768]{2,1,0:T(8,128)(2,1)} %get-tuple-element.59.att_in, bf16[2,512,768]{2,1,0:T(8,128)(2,1)} %get-tuple-element.60.datt_in, ...), custom_call_target="tpu_custom_call" | custom-call | tf_op jit(solution)/shard_map/finish/pallas_call | solution.py:1376
  258.4 0.0 copy-done.5
  258.4 0.0 copy-done.6
  258.4 0.0 copy-done.7
  258.5 1.4 multiply_subtract_fusion.1
  259.8 3.8 %conditional.3 = (f32[221184]{0:T(1024)S(1)}) conditional(s32[]{:T(128)} %clamp.4, f32[288,768]{1,0:T(8,128)S(1)} %get-tuple-element.72, f32[288,768]{1,0:T(8,128)S(1)} %get-tuple-element.72, f32[288,768]{1,0:T(8,128)S(1)} %get-tuple-element.72, f32[288,768]{1,0:T(8,128)S(1)} %get-tuple-element.72, ...), branch_computations={%region_6.0_spmd, %region_7.0_spmd, %region_8.0_spmd, %region_9.0_... | conditional | flops 221184 | bytes 6488072 | solution.py:109
  259.8 1.5 reshape.86
  261.3 1.9 copy.28
  263.2 0.5 reshape.87
  263.7 0.0 copy-start
  263.7 0.0 copy-start.2
  263.7 0.0 copy-start.3
  263.7 3.5 %convert_element_type.62 = f32[8,128,768]{2,1,0:T(8,128)} convert(bf16[8,128,768]{2,1,0:T(8,128)(2,1)} %get-tuple-element.71) | non-fusion elementwise | flops 786432 | bytes 4718592 | tf_op jit(solution)/shard_map/convert_element_type | solution.py:1520
  267.2 0.0 copy-done
  267.2 0.0 copy-done.2
  267.2 0.0 copy-done.3
  267.2 0.0 copy-start.1
  267.2 1.9 multiply_subtract_fusion
  269.2 0.0 copy-done.1
  269.2 1.1 copy.51
  (1 shorter events, 0.0 us)
Async XLA Ops:
  1.5 1.6 copy-start.4
  141.0 117.4 %copy-start.5 = (f32[288]{0:T(512)S(1)}, f32[288]{0:T(512)}, u32[]{:S(2)}) copy-start(f32[288]{0:T(512)} %param.29) | copy-start | bytes 3460
  141.1 117.4 %copy-start.6 = (f32[288]{0:T(512)S(1)}, f32[288]{0:T(512)}, u32[]{:S(2)}) copy-start(f32[288]{0:T(512)} %param.30) | copy-start | bytes 3460
  141.1 117.4 %copy-start.7 = (f32[288]{0:T(512)S(1)}, f32[288]{0:T(512)}, u32[]{:S(2)}) copy-start(f32[288]{0:T(512)} %param.31) | copy-start | bytes 3460
  263.7 3.5 %copy-start = (f32[221184]{0:T(1024)S(1)}, f32[221184]{0:T(1024)}, u32[]{:S(2)}) copy-start(f32[221184]{0:T(1024)} %param.26) | copy-start | bytes 2654212
  263.7 3.5 %copy-start.2 = (f32[221184]{0:T(1024)S(1)}, f32[221184]{0:T(1024)}, u32[]{:S(2)}) copy-start(f32[221184]{0:T(1024)} %param.27) | copy-start | bytes 2654212
  263.7 3.5 %copy-start.3 = (f32[221184]{0:T(1024)S(1)}, f32[221184]{0:T(1024)}, u32[]{:S(2)}) copy-start(f32[221184]{0:T(1024)} %param.28) | copy-start | bytes 2654212
  267.2 1.9 copy-start.1

commit v2 on v1

--- a/solution.py
+++ b/solution.py
@@ -190,6 +190,35 @@
             lambda: dispatch(now, steps[:middle], body),
             lambda: dispatch(now, steps[middle:], body),
         )
+
+
+def share_layouts(shares, rows):
+    found = []
+    for share in range(shares):
+        layout = [(name, pieces, at, size) for name, pieces, at, _, size in segments(share, rows)]
+        if not found or found[-1][1] != layout:
+            found.append((share, layout))
+    return found
+
+
+def for_share(number, shares, rows, body):
+    layouts = share_layouts(shares, rows)
+    for (begin, layout), end in zip(layouts, [begin for begin, _ in layouts[1:]] + [shares]):
+        pl.when(jnp.logical_and(number >= begin, number < end))(functools.partial(body, layout))
+
+
+def share_blocks(layout):
+    per = D // 128
+    for name, pieces, at, size in layout:
+        each = size // pieces
+        for j in range(pieces):
+            for k in range(per):
+                flat = pl.ds((at + j) * per + k, each, stride=per * pieces)
+                if name == "qkv":
+                    row, column = at + k // 2 * each, j * (D // 3) + k % 2 * 128
+                else:
+                    row, column = at + j * each, k * 128
+                yield flat, slice(row, row + each), slice(column, column + 128)
 
 
 class Sends:
@@ -363,10 +392,10 @@
     2: (("q", 2, 1), ("q_start", 2), ("q", 3, 1), ("q", 1, 2), ("q", 4, 1), ("q", 2, 2), ("q", 3, 2), ("q", 4, 2)),
 }
 TIMES = {
-    0: dict(then=(0, 3, 4, 9, 89), far=(37, 49, 58, 66, 74), across=(0, 25, 30, 64, 80), dy=33),
-    1: dict(own=(-1, 18, 24, 56, 64), over_x=0, far=(34, 43, 68, 76, 83), dy=27),
-    2: dict(then=(0, 0, 0, 0, 11, 12, 17, 84), own=(1, 18, 27, 49, 57), over_x=0, dy=64),
-    3: dict(own=(59, 69, 75, 83, 85), over_x=2, far=(3, 28, 43, 68, 76), across=(16, 23, 53, 56, 89), dy=21),
+    0: dict(then=(0, 15, 27, 69, 84), far=(28, 36, 52, 68, 79), across=(11, 17, 32, 33, 77), dy=27),
+    1: dict(own=(3, 18, 29, 33, 49), over_x=4, far=(30, 47, 64, 76, 82), dy=23),
+    2: dict(then=(0, 2, 3, 6, 13, 13, 67, 71), own=(-1, 26, 42, 52, 60), over_x=0, dy=63),
+    3: dict(own=(21, 66, 73, 84, 89), over_x=17, far=(9, 38, 53, 63, 75), across=(0, 0, 7, 11, 82), dy=72),
 }
 
 
@@ -406,9 +435,9 @@
 
 
 def forward_kernel(
-    n_batch, plan, share, vec, x_in, grad_in, scored, mask,
+    n_batch, plan, flat, vec, x_in, grad_in, scored, mask,
     mats, x_out, qkv_out, att_out, lse_out, out_own, dr1_out, datt_out, act_out, du_out, h1_out, dz_out, da_out, sums,
-    x_all, att, dy, dy_in, out, wide, datt, w_out, w_up, w_down, stage, act, act_t, slope, h1_t, dz, da, scales, biases, lse, masks, vecs, vec_in,
+    x_all, att, dy, dy_in, out, share_wide, share, wide, datt, w_out, w_up, w_down, stage, act, act_t, slope, h1_t, dz, da, scales, biases, lse, masks, vecs, vec_in,
     own_sem, send_sem, mat_sem, vec_sem, seq_sem, w_sem, mask_sem, out_sem, load_sem, stage_sem, row_sem, give_sem, give_own, grad_sem,
 ):
     at = Place(n_batch)
@@ -420,6 +449,7 @@
     seqs, length = x_all.shape[:2]
     depth = share.shape[1]
     n_up = FF // D
+    shares = mats.shape[0]
     mine = pl.ds(at.seq * tokens, tokens)
     w, qkv = w_up, slope
 
@@ -433,12 +463,21 @@
     for i in range(grad_in.shape[0]):
         there = wide.at[i // per_row, pl.ds(i % per_row * tokens, tokens)]
         grads.append(pltpu.make_async_copy(grad_in.at[i], there, grad_sem.at[i]))
-    for copy in own[:2] + grads:
+    for copy in own[1:2] + grads:
         copy.start()
 
     for unit in range(2):
         pltpu.make_async_copy(mask.at[unit], masks.at[unit], mask_sem.at[unit]).start()
     vecs[...] = vec[...]
+
+    def from_flat_order(layout):
+        for flat_rows, lines, lanes in share_blocks(layout):
+            share_wide[lines, lanes] = flat[flat_rows, :]
+
+    for_share(at.seq * n_batch + at.batch, shares, 3 * depth, from_flat_order)
+    for piece in range(3):
+        share[piece] = share_wide[piece * depth : (piece + 1) * depth, :].astype(BF16)
+    own[0].start()
     at.barrier()
 
     all_of = (0, 3, 0)
@@ -909,8 +948,8 @@
     sends.drain(at.core_peer)
 
 
-def forward(n_batch, share, vec, x_in, grad_in, scored, mask):
-    rows = share.shape[0]
+def forward(n_batch, flat, vec, x_in, grad_in, scored, mask):
+    rows = flat.shape[0] * 128 // D
     depth = rows // 3
     shares = 4 * n_batch
     n_z = n_batch // 2
@@ -923,9 +962,8 @@
             if name != "qkv":
                 plan.append((name, number, at, begin, size))
     whole, low, gelu = (seqs, length, D), (D, tokens), (n_up, seqs, length, D)
-    share = share.reshape(3, depth, D)
     outs = [
-        ((shares,) + share.shape, BF16),
+        ((shares, 3, depth, D), BF16),
         (whole, BF16),
         ((3,) + whole, BF16),
         (whole, BF16),
@@ -946,6 +984,8 @@
         (whole, BF16),
         (x_in.shape, BF16),
         (whole, BF16),
+        ((rows, D), F32),
+        ((3, depth, D), BF16),
         (whole, F32),
         (whole, BF16),
         ((D // depth, depth, D), BF16),
@@ -970,7 +1010,7 @@
     return pl.pallas_call(
         functools.partial(forward_kernel, n_batch, plan),
         out_shape=[jax.ShapeDtypeStruct(shape, dtype) for shape, dtype in outs],
-        in_specs=[ANY, VMEM, ANY, ANY, VMEM, ANY],
+        in_specs=[VMEM, VMEM, ANY, ANY, VMEM, ANY],
         out_specs=[ANY] * 13 + [VMEM],
         scratch_shapes=[pltpu.VMEM(shape, dtype) for shape, dtype in vmem]
         + [pltpu.SemaphoreType.DMA(shape) for shape in sems],
@@ -978,15 +1018,15 @@
             collective_id=0, has_side_effects=True, vmem_limit_bytes=60 * MIB
         ),
         name="forward",
-    )(share, vec, x_in, grad_in, scored, mask)
+    )(flat, vec, x_in, grad_in, scored, mask)
 
 
 PLACES = (4, 3, -3, 2, -2, 1, -1, 0)
 REDUCE_TIMES = {
-    0: dict(over_x=(-2, -2, 0, 14, 8, 13, 8, 17), late=((5, 13, 16, 26, 28, 28), (16, 19, 22, 24, 28, 28), (3, 3, 5, 27, 28, 28))),
-    1: dict(kind0=(9, 20, 27, 28, 28), kind1=(0, 5, 9, 15, 17, 22)),
-    2: dict(kind0=(5, 9, 25, 27, 28), late=((12, 14, 16, 17, 21, 28), (16, 18, 21, 24, 25, 25), (16, 16, 25, 26, 27, 28))),
-    3: dict(over_x=(4, 7, 7, 17, 9, 12, 11, 17), kind1=(0, 6, 10, 19, 27, 27)),
+    0: dict(over_x=(-2, 0, -2, 13, 6, 21, 16, 6), late=((6, 15, 16, 22, 26, 28), (20, 23, 27, 28, 28, 28), (6, 26, 27, 27, 28, 28))),
+    1: dict(kind0=(11, 18, 25, 28, 28), kind1=(-2, -1, 5, 8, 14, 22)),
+    2: dict(kind0=(6, 12, 21, 27, 28), late=((3, 11, 21, 25, 27, 27), (3, 20, 23, 25, 28, 28), (4, 26, 27, 27, 28, 28))),
+    3: dict(over_x=(4, 7, 13, 17, 6, 20, 6, 21), kind1=(-2, 1, 11, 17, 28, 28)),
 }
 
 
@@ -1011,7 +1051,7 @@
 def finish_kernel(
     n_batch, mask, qkv_in, att_in, datt_in, lse_in, x_in, mats, dr1_in, act_in, du_in, h1_in, dz_in, da_in, sums,
     share, vec_out, dx_own,
-    qkv, att, datt, lse, w, wide, dqkv, dx, turned, act_t, masks, probs, dscore, grads, from_core, x_a, ring_in, x_b, vec_in,
+    qkv, att, datt, lse, w, wide, dqkv, dx, act_t, masks, probs, dscore, grads, from_core, x_a, ring_in, x_b, total, vec_in,
     in_sem, mask_sem, act_sem, du_sem, own_sem, send_sem, core_sem, a_sem, ring_sem, b_sem, vec_sem, seq_sem,
 ):
     at = Place(n_batch)
@@ -1025,11 +1065,12 @@
     sends = Sends(send_sem)
     mine = pl.ds(at.seq * tokens, tokens)
     dz, da, x = dqkv.at[2], dx, dx
+    turned, h1_t = act_t.at[0], act_t.at[1]
 
     ins = [
         pltpu.make_async_copy(src, dst, in_sem.at[i])
         for i, (src, dst) in enumerate(
-            ((dz_in, dz), (att_in, att), (h1_in, turned), (da_in, da), (qkv_in, qkv), (datt_in, datt), (lse_in, lse))
+            ((dz_in, dz), (att_in, att), (da_in, da), (qkv_in, qkv), (datt_in, datt), (lse_in, lse))
         )
     ]
 
@@ -1109,14 +1150,18 @@
         if kind == 0 and is_own(seq, 0):
             sends.arrived(x_a.at[b], a_sem.at[b], at.core_peer)
 
+    def slot(way, hops):
+        return 1 + way * (half - 1) + hops - 1 if hops else 0
+
     def ring_send(kind, b, way, hops, part):
         peer = (at.next, at.prev)[way]
         lines = part_rows(part)
-        sends.start(from_core.at[kind, b, lines], ring_in.at[kind, way, hops, lines], ring_sem.at[kind, way, hops, part[0]], peer, lambda: ring_in.at[0, 0, 0, lines])
+        sends.start(from_core.at[kind, b, lines], ring_in.at[kind, slot(way, hops), lines], ring_sem.at[kind, way, hops, part[0]], peer, lambda: ring_in.at[0, 0, lines])
 
     def ring_wait(kind, way, hops, part):
-        sends.arrived(ring_in.at[kind, way, hops, part_rows(part)], ring_sem.at[kind, way, hops, part[0]], at.core_peer)
-        return ring_in.at[kind, way, hops]
+        here = ring_in.at[kind, slot(way, hops)]
+        sends.arrived(here.at[part_rows(part)], ring_sem.at[kind, way, hops, part[0]], at.core_peer)
+        return here
 
     def ring_step(seq, kind, piece, what, hops=0):
         own = is_own(seq, kind)
@@ -1145,14 +1190,14 @@
             b = at.batch
             ready(seq, kind, b, piece)
             others = [ring_wait(kind, way, half - 1, whole) for way in range(2)]
-            add(seq, kind, b, whole, *others, into=share if own else None)
+            add(seq, kind, b, whole, *others, into=total if own else None)
             if not own:
                 lines = part_rows(whole)
                 sends.start(from_core.at[kind, b, lines], x_b.at[lines], b_sem.at[whole[0]], at.x_peer, lambda: x_b.at[lines])
         elif own:
             far_part = ring_of(False, kind, piece)[0]
             sends.arrived(x_b.at[part_rows(far_part)], b_sem.at[far_part[0]], at.core_peer)
-            add_rows(share, (far_part[0] * depth, (far_part[1] - far_part[0]) * depth), (x_b, far_part[0] * depth))
+            add_rows(total, (far_part[0] * depth, (far_part[1] - far_part[0]) * depth), (x_b, far_part[0] * depth))
 
     def over_x(seq, step):
         b = at.around(step)
@@ -1206,9 +1251,11 @@
             fetch_act(down_order[number + 2]).start()
         if number == n_up - 2:
             sends.under(on_core[0], functools.partial(to_core, 0, 1))
+            h1_copy = pltpu.make_async_copy(h1_in, h1_t, in_sem.at[9 + n_batch])
+            h1_copy.start()
     put_vec(starts[4], contract(ones, flat(dz[...]), (1, 0)))
     reduce_at(-3)
-    ins[2].wait()
+    h1_copy.wait()
     ups = []
     for number in range(4 * n_batch):
         ups += [(number, at_row, begin, size) for name, _, at_row, begin, size in segments(number, rows) if name == "up"]
@@ -1218,7 +1265,7 @@
             for k in range(2):
                 j = pair * 2 + k
                 fetch_du(j).wait()
-                wide[k, 0:middle] = contract(turned[high * middle : (high + 1) * middle], flat(dqkv[j % 2]), (1, 0))
+                wide[k, 0:middle] = contract(h1_t[high * middle : (high + 1) * middle], flat(dqkv[j % 2]), (1, 0))
                 if high:
                     put_vec(starts[3] + j * per, contract(ones, flat(dqkv[j % 2]), (1, 0)))
                 if not (high == 0 and pair == n_up // 2 - 1):
@@ -1233,7 +1280,7 @@
             sends.under(on_core[1], functools.partial(to_core, 1, 0))
             reduce_at(-2)
     ins[1].wait()
-    ins[3].wait()
+    ins[2].wait()
     for seq in range(seqs):
         turned[:, seq * length : (seq + 1) * length] = att[seq].T
     for i in range(D // block):
@@ -1247,7 +1294,7 @@
     dr1_copy.start()
     x_copy = pltpu.make_async_copy(x_in, x, in_sem.at[7])
     x_copy.start()
-    for copy in ins[4:]:
+    for copy in ins[3:]:
         copy.wait()
     x_copy.wait()
     for seq in range(seqs):
@@ -1265,9 +1312,9 @@
         for j in range(3):
             right = dqkv[j, :, :, lanes].reshape(seqs * length, width)
             for i in range(D // lines):
-                total = contract(turned[i * lines : (i + 1) * lines], right, (1, 0)).astype(BF16)
+                values = contract(turned[i * lines : (i + 1) * lines], right, (1, 0)).astype(BF16)
                 for k in range(4):
-                    grads[0, 4 * i + k, piece * depth : (piece + 1) * depth, j * width : (j + 1) * width] = total[k * depth : (k + 1) * depth]
+                    grads[0, 4 * i + k, piece * depth : (piece + 1) * depth, j * width : (j + 1) * width] = values[k * depth : (k + 1) * depth]
         sends.under(on_core[1], functools.partial(to_core, 1, 1, (piece, piece + 1)))
 
     def one_head(head, carry):
@@ -1309,12 +1356,12 @@
         reduce_at(units + number)
         theirs = pl.ds(pl.multiple_of(at.seq_at(step) * tokens, tokens), tokens)
         for seq in range(seqs):
-            total = wide[seq, theirs]
+            value = wide[seq, theirs]
             for j in range(3):
                 for piece in range(3):
                     left = dqkv[j, seq, theirs, piece * width : (piece + 1) * width]
-                    total = total + contract(left, w[piece, :, j * width : (j + 1) * width], (1, 1))
-            dx[seq, theirs] = total.astype(BF16)
+                    value = value + contract(left, w[piece, :, j * width : (j + 1) * width], (1, 1))
+            dx[seq, theirs] = value.astype(BF16)
         there = dx_own.at[pl.ds(at.seq * seqs, seqs)]
         if step:
             sends.start(dx.at[:, theirs], there, seq_sem.at[step], at.seq_peer(step), lambda: dx.at[:, pl.ds(0, tokens)])
@@ -1331,6 +1378,12 @@
     for step in range(1, n_z):
         sends.start(vec_in.at[2 * n_z + 2], vec_in.at[2 + 2 * n_z + step], vec_sem.at[3 + step], at.z_peer(step))
     reduce_at(units + 5)
+
+    def in_flat_order(layout):
+        for flat_rows, lines, lanes in share_blocks(layout):
+            share[flat_rows, :] = total[lines, lanes]
+
+    for_share(at.seq * n_batch + at.batch, 4 * n_batch, rows, in_flat_order)
     for step in range(1, n_z):
         slot_in = 2 + 2 * n_z + step
         sends.arrived(vec_in.at[slot_in], vec_sem.at[3 + step], at.core_peer)
@@ -1349,7 +1402,6 @@
     n_z = n_batch // 2
     seqs = att.shape[0]
     whole = (att.shape, BF16)
-    turned = (D, seqs * length)
     vec = (sum(VEC_LENGTHS) // 128, 128)
     vmem = [
         (qkv.shape, BF16),
@@ -1360,23 +1412,23 @@
         (att.shape, F32),
         (qkv.shape, BF16),
         whole,
-        (turned, BF16),
-        ((2,) + turned, BF16),
+        ((2, D, seqs * length), BF16),
         ((2, length, length), jnp.int32),
         ((length, length), BF16),
         ((length, length), BF16),
         ((4, n_batch, rows, D), BF16),
         ((2, n_batch, rows, D), BF16),
         ((n_batch, rows, D), BF16),
-        ((2, 2, n_z, rows, D), BF16),
+        ((2, 2 * n_z - 1, rows, D), BF16),
         ((rows, D), BF16),
+        ((rows, D), F32),
         ((3 * n_z + 3,) + vec, F32),
     ]
-    sems = [(9 + n_batch,), (2,), (2,), (2,), (1,), (400,), (2, n_batch, 3), (n_batch,), (2, 2, n_z, 3), (3,), (n_z + 3,), (4,)]
+    sems = [(10 + n_batch,), (2,), (2,), (2,), (1,), (400,), (2, n_batch, 3), (n_batch,), (2, 2, n_z, 3), (3,), (n_z + 3,), (4,)]
     return pl.pallas_call(
         functools.partial(finish_kernel, n_batch),
         out_shape=(
-            jax.ShapeDtypeStruct((rows, D), F32),
+            jax.ShapeDtypeStruct((rows * D // 128, 128), F32),
             jax.ShapeDtypeStruct(vec, F32),
             jax.ShapeDtypeStruct((seqs * 4, length // 4, D), BF16),
         ),
@@ -1478,18 +1530,19 @@
     vec_len = vec_param.shape[0]
     me = lax.axis_index("seq") * n_batch + lax.axis_index("batch")
 
-    share = rearrange(me, shares, mat_param.reshape(share_rows, D).astype(BF16), by_columns)
     vec_share = lax.dynamic_update_slice(
         jnp.zeros((shares * vec_len,), F32), vec_param.astype(BF16).astype(F32), (me * vec_len,)
     ).reshape(-1, 128)
     if share_rows % 96 == 0 and share_rows * n_batch == 3 * D:
         mats, x_all, qkv, attended, lse, outputs, *middle = forward(
-            n_batch, share, vec_share, inputs, out_grad, out_mask, attn_mask
+            n_batch, mat_param.reshape(-1, 128), vec_share, inputs, out_grad, out_mask, attn_mask
         )
         dr1, datt, *middle = middle
         mat_grad, vec_sum, dx = finish(n_batch, attn_mask, qkv, attended, datt, lse, x_all, mats, dr1, *middle)
+        mat_grad = mat_grad.reshape(-1)
         vec_grad = lax.dynamic_slice_in_dim(vec_sum.reshape(-1), me * vec_len, vec_len)
     else:
+        share = rearrange(me, shares, mat_param.reshape(share_rows, D).astype(BF16), by_columns)
         mats = lax.all_gather(share, ("seq", "batch"))
         vecs = lax.psum(vec_share, ("seq", "batch")).reshape(-1)
         dy_low = (out_grad * out_mask[..., None].astype(F32)).astype(BF16)
@@ -1510,11 +1563,11 @@
         mats_grad["qkv"] = regroup(mats_grad["qkv"])
         grads = to_shares({name: part.astype(BF16) for name, part in mats_grad.items()}, shares)
         mat_grad = lax.psum_scatter(grads.astype(F32), ("seq", "batch"))
+        mat_grad = rearrange(me, shares, mat_grad, by_rows).reshape(-1)
         vec_grad = lax.psum_scatter(jnp.concatenate([db, grad_vecs]), ("seq", "batch"), tiled=True)
         outputs, dx = (
             lax.all_to_all(member, "seq", 1, 0, tiled=True) for member in (out_all.reshape(whole), dx_all)
         )
-    mat_grad = rearrange(me, shares, mat_grad, by_rows).reshape(-1)
     return (
         outputs,
         dx.astype(F32),

time: 274 us -> 270 us (0.985)
  local copies, waits for them, and re-layouts: 6.34 us -> 1.8 us
    pallas_call x1, Pallas kernels: 117 us -> 110 us  [finish(): pl.pallas_call(functools.partial(finish_kernel, n_batch), out_shape=(jax....]
    pallas_call x1, Pallas kernels: 137 us -> 144 us  [forward(): pl.pallas_call(functools.partial(forward_kernel, n_batch, plan), out_shap...]
where the time goes in v2:
time: 270 us; the launch traced here: 265 us
  Pallas kernels  254 us (94%)
  other arithmetic  7.6 us (3%)
    pallas_call x1, Pallas kernels, forward(): pl.pallas_call(functools.partial(forward_kernel, n_batch, plan), out_shap...  144 us
    pallas_call x1, Pallas kernels, finish(): pl.pallas_call(functools.partial(finish_kernel, n_batch), out_shape=(jax....  110 us

profile of v2, /device:TPU:0, one launch (start us, length us, event | category | flops | bytes accessed | tf_op | source)
XLA Modules:
  0.0 264.5 jit_solution(10151071421752982435)
XLA Ops:
  0.7 0.8 convert_dynamic-update-slice_fusion
  1.5 0.0 copy-start.5
  1.5 0.6 copy-done.5
  2.1 143.7 %forward.1 = (bf16[32,3,96,768]{3,2,1,0:T(8,128)(2,1)}, bf16[2,512,768]{2,1,0:T(8,128)(2,1)}, bf16[3,2,512,768]{3,2,1,0:T(8,128)(2,1)}, bf16[2,512,768]{2,1,0:T(...) custom-call(f32[1728,128]{1,0:T(8,128)} %bitcast.10, ...), custom_call_target="tpu_custom_call" | custom-call | tf_op jit(solution)/shard_map/forward/pallas_call | solution.py:1010
  145.8 0.0 copy-start.6
  145.8 0.0 copy-start.7
  145.8 0.0 copy-start.8
  145.8 110.4 %finish.1 = (f32[1728,128]{1,0:T(8,128)}, f32[72,128]{1,0:T(8,128)}, bf16[8,128,768]{2,1,0:T(8,128)(2,1)}) custom-call(s32[12,512,512]{2,1,0:T(8,128)} %mask.3, bf16[3,2,512,768]{3,2,1,0:T(8,128)(2,1)} %get-tuple-element.26.qkv_in, bf16[2,512,768]{2,1,0:T(8,128)(2,1)} %get-tuple-element.27.att_in, bf16[2,512,768]{2,1,0:T(8,128)(2,1)} %get-tuple-element.28.datt_in, ...), custom_call_target="tpu_custom_call" | custom-call | tf_op jit(solution)/shard_map/finish/pallas_call | solution.py:1428
  256.2 0.0 copy-done.6
  256.2 0.0 copy-done.7
  256.3 0.0 copy-done.8
  256.3 1.4 multiply_subtract_fusion.1
  257.6 0.0 copy-start
  257.6 0.0 copy-start.2
  257.7 0.0 copy-start.3
  257.7 0.0 copy-start.4
  257.7 3.5 %convert_element_type.11 = f32[8,128,768]{2,1,0:T(8,128)} convert(bf16[8,128,768]{2,1,0:T(8,128)(2,1)} %get-tuple-element.39) | non-fusion elementwise | flops 786432 | bytes 4718592 | tf_op jit(solution)/shard_map/convert_element_type | solution.py:1573
  261.2 0.0 copy-done
  261.2 0.0 copy-done.2
  261.2 0.0 copy-done.3
  261.2 0.0 copy-done.4
  261.2 0.0 copy-start.1
  261.2 1.9 multiply_subtract_fusion
  263.1 0.0 copy-done.1
  263.1 1.1 copy.20
  (1 shorter events, 0.0 us)
Async XLA Ops:
  1.5 0.6 copy-start.5
  145.8 110.5 %copy-start.6 = (f32[288]{0:T(512)S(1)}, f32[288]{0:T(512)}, u32[]{:S(2)}) copy-start(f32[288]{0:T(512)} %param.17) | copy-start | bytes 3460
  145.8 110.5 %copy-start.7 = (f32[288]{0:T(512)S(1)}, f32[288]{0:T(512)}, u32[]{:S(2)}) copy-start(f32[288]{0:T(512)} %param.18) | copy-start | bytes 3460
  145.8 110.5 %copy-start.8 = (f32[288]{0:T(512)S(1)}, f32[288]{0:T(512)}, u32[]{:S(2)}) copy-start(f32[288]{0:T(512)} %param.19) | copy-start | bytes 3460
  257.6 3.5 %copy-start = (f32[221184]{0:T(1024)S(1)}, f32[221184]{0:T(1024)}, u32[]{:S(2)}) copy-start(f32[221184]{0:T(1024)} %param.14) | copy-start | bytes 2654212
  257.6 3.5 %copy-start.2 = (f32[221184]{0:T(1024)S(1)}, f32[221184]{0:T(1024)}, u32[]{:S(2)}) copy-start(f32[221184]{0:T(1024)} %param.15) | copy-start | bytes 2654212
  257.7 3.5 %copy-start.3 = (f32[221184]{0:T(1024)S(1)}, f32[221184]{0:T(1024)}, u32[]{:S(2)}) copy-start(f32[221184]{0:T(1024)} %param.16) | copy-start | bytes 2654212
  257.7 3.5 %copy-start.4 = (f32[1728,128]{1,0:T(8,128)S(1)}, f32[1728,128]{1,0:T(8,128)}, u32[]{:S(2)}) copy-start(f32[1728,128]{1,0:T(8,128)} %get-tuple-element.40) | copy-start | bytes 2654212
  261.2 1.9 copy-start.1
